TPU v7x, 32 devices: a whole 2x2x4 slice. The times are simulated.
32 devices in a mesh: lon: 16 (over z, y, core), lat: 2 (over x).
Axes of the slice: x: 2, y: 2, z: 4, core: 2. Of those that a mesh axis runs over, the one named last changes fastest.
Arguments:
- prediction: bfloat16 [96, 384, 222], P('lat', 'lon'), may hold values from -40 to 40
- observed_state: bfloat16 [96, 384, 222], P('lat', 'lon'), may hold values from -40 to 40
- mean_state: bfloat16 [96, 384, 222], P('lat', 'lon'), may hold values from -6 to 6
- usable_point_flags: int32 [96, 384], P('lat', 'lon'), may hold values 0 or 1
- eastward_offsets: int32 [8], replicated, may hold values from 0 to 335, as said below
Outputs:
- correlation: float32 [8, 384, 222], P('lat', 'lon')
Inputs may be any that keep to these rules, and one draw needn't show every extreme that they name: `eastward_offsets`: every lag lies below 336, and some lag equals 335.
All inputs are finite; a program needn't handle non-finite values. No bound on the sum of `usable_point_flags` on one device may be relied on, other than what follows from the above.
Results may differ from a plain program's by a relative error of at most 0.0044.
Values may be sent and summed in bfloat16 or wider, within the bound.
A program may use at most 64 MiB of HBM per device.

v0:
```python
import jax
import jax.numpy as jnp
from jax import lax
from jax.sharding import PartitionSpec as P

REACH = 14


regular_term = 0.001


def from_behind(value, axis, by):
    count = lax.axis_size(axis)
    return lax.ppermute(value, axis, [(i, (i + by) % count) for i in range(count)])


def local(prediction, observed_state, mean_state, usable_point_flags, eastward_offsets):
    meridian_extent, parallel_extent, field_total = prediction.shape
    total_rows = meridian_extent * lax.axis_size("lat")
    row_index = (
        lax.axis_index("lat") * meridian_extent + jnp.arange(meridian_extent, dtype=jnp.int32)
    ).astype(jnp.float32)
    weights = jnp.cos(jnp.pi * ((row_index + 0.5) / total_rows - 0.5))
    predicted_mean_state = mean_state.astype(jnp.float32)
    prediction_departure = prediction.astype(jnp.float32) - predicted_mean_state
    observed_departure = (observed_state.astype(jnp.float32) - predicted_mean_state).astype(
        jnp.bfloat16
    )
    base_weight = weights[:, None] * usable_point_flags.astype(jnp.float32)
    window_cols = (REACH + 1) * parallel_extent
    start_true = jnp.zeros((meridian_extent, window_cols, field_total), jnp.bfloat16)
    start_true = lax.dynamic_update_slice_in_dim(start_true, observed_departure, 0, 1)
    start_valid = jnp.zeros((meridian_extent, window_cols), jnp.int32)
    start_valid = lax.dynamic_update_slice_in_dim(start_valid, usable_point_flags, 0, 1)

    def advance(turn_index, state_tuple):
        buffer_true, buffer_valid, slab_true, slab_valid = state_tuple
        slab_true, slab_valid = from_behind((slab_true, slab_valid), "lon", -1)
        place = (turn_index + 1) * parallel_extent
        buffer_true = lax.dynamic_update_slice_in_dim(buffer_true, slab_true, place, 1)
        buffer_valid = lax.dynamic_update_slice_in_dim(buffer_valid, slab_valid, place, 1)
        return (buffer_true, buffer_valid, slab_true, slab_valid)

    win_true, win_valid, unused_true, unused_valid = lax.fori_loop(
        0, REACH, advance, (start_true, start_valid, observed_departure, usable_point_flags)
    )

    def lag_sums(offset):
        frame_segment = lax.dynamic_slice_in_dim(win_true, offset, parallel_extent, 1).astype(
            jnp.float32
        )
        piece_valid = lax.dynamic_slice_in_dim(win_valid, offset, parallel_extent, 1).astype(
            jnp.float32
        )
        couple_factor = (base_weight * piece_valid)[:, :, None]
        joint_moment = jnp.sum(couple_factor * prediction_departure * frame_segment, axis=0)
        prediction_spread = jnp.sum(
            couple_factor * prediction_departure * prediction_departure, axis=0
        )
        var_true = jnp.sum(couple_factor * frame_segment * frame_segment, axis=0)
        return (joint_moment, prediction_spread, var_true)

    joint_moment, prediction_spread, var_true = lax.map(lag_sums, eastward_offsets)
    joint_moment, prediction_spread, var_true = (
        lax.psum_scatter(joint_moment, "lat", scatter_dimension=0, tiled=True),
        lax.psum_scatter(prediction_spread, "lat", scatter_dimension=0, tiled=True),
        lax.psum_scatter(var_true, "lat", scatter_dimension=0, tiled=True),
    )
    return joint_moment / jnp.sqrt((prediction_spread + regular_term) * (var_true + regular_term))


def solution(mesh):
    placed = (
        P("lat", "lon", None),
        P("lat", "lon", None),
        P("lat", "lon", None),
        P("lat", "lon"),
        P(),
    )
    return jax.shard_map(
        local, mesh=mesh, in_specs=placed, out_specs=P("lat", "lon", None), check_vma=False
    )
```

profile of v0, /device:TPU:0, one launch (start us, length us, event | category | flops | bytes accessed | tf_op | source)
XLA Modules:
  0.0 293.4 jit_solution(4611384276423056334)
XLA Ops:
  13.2 193.1 %while.33 = (s32[]{:T(128)}, bf16[48,360,222]{2,1,0:T(8,128)(2,1)}, s32[48,360]{1,0:T(8,128)S(1)}, bf16[48,24,222]{2,1,0:T(8,128)(2,1)S(1)}, s32[48,24]{1,0:T(8,...) while((s32[]{:T(128)}, bf16[48,360,222]{2,1,0:T(8,128)(2,1)}, s32[48,360]{1,0:T(8,128)S(1)}, ...), condition=%wide.region_1.0_spmd, body=%wide.region_0.0_spmd.sunk | while | flops 6 | bytes 4207331 | solution.py:44
  13.2 5.4 %collective-permute-start = (bf16[48,24,222]{2,1,0:T(8,128)(2,1)S(1)}, bf16[48,24,222]{2,1,0:T(8,128)(2,1)S(1)}, u32[]{:S(2)}, u32[]{:S(2)}) collective-permute-start(bf16[48,24,222]{2,1,0:T(8,128)(2,1)S(1)} %get-tuple-element.302), channel_id=1, source_target_pairs={{0,30},{2,0},{4,2},{6,4},{8,6},{10,8},{12,10},{14,12},{16,14},{18,... | collective-permute-start | bytes 1534472 | tf_op jit(solution)/shard_map/while/body/eval_jaxpr/ppermute | solution.py:14
  19.3 7.0 %collective-permute-done.1 = s32[48,24]{1,0:T(8,128)S(1)} collective-permute-done((s32[48,24]{1,0:T(8,128)S(1)}, s32[48,24]{1,0:T(8,128)S(1)}, u32[]{:S(2)}, u32[]{:S(2)}) %collective-permute-start.1) | collective-permute-done | bytes 4640 | tf_op jit(solution)/shard_map/while/body/eval_jaxpr/ppermute | solution.py:14
  27.8 4.6 %collective-permute-start = (bf16[48,24,222]{2,1,0:T(8,128)(2,1)S(1)}, bf16[48,24,222]{2,1,0:T(8,128)(2,1)S(1)}, u32[]{:S(2)}, u32[]{:S(2)}) collective-permute-start(bf16[48,24,222]{2,1,0:T(8,128)(2,1)S(1)} %get-tuple-element.302), channel_id=1, source_target_pairs={{0,30},{2,0},{4,2},{6,4},{8,6},{10,8},{12,10},{14,12},{16,14},{18,... | collective-permute-start | bytes 1534472 | tf_op jit(solution)/shard_map/while/body/eval_jaxpr/ppermute | solution.py:14
  32.5 7.6 %collective-permute-done.1 = s32[48,24]{1,0:T(8,128)S(1)} collective-permute-done((s32[48,24]{1,0:T(8,128)S(1)}, s32[48,24]{1,0:T(8,128)S(1)}, u32[]{:S(2)}, u32[]{:S(2)}) %collective-permute-start.1) | collective-permute-done | bytes 4640 | tf_op jit(solution)/shard_map/while/body/eval_jaxpr/ppermute | solution.py:14
  46.2 7.6 %collective-permute-done.1 = s32[48,24]{1,0:T(8,128)S(1)} collective-permute-done((s32[48,24]{1,0:T(8,128)S(1)}, s32[48,24]{1,0:T(8,128)S(1)}, u32[]{:S(2)}, u32[]{:S(2)}) %collective-permute-start.1) | collective-permute-done | bytes 4640 | tf_op jit(solution)/shard_map/while/body/eval_jaxpr/ppermute | solution.py:14
  55.3 4.6 %collective-permute-start = (bf16[48,24,222]{2,1,0:T(8,128)(2,1)S(1)}, bf16[48,24,222]{2,1,0:T(8,128)(2,1)S(1)}, u32[]{:S(2)}, u32[]{:S(2)}) collective-permute-start(bf16[48,24,222]{2,1,0:T(8,128)(2,1)S(1)} %get-tuple-element.302), channel_id=1, source_target_pairs={{0,30},{2,0},{4,2},{6,4},{8,6},{10,8},{12,10},{14,12},{16,14},{18,... | collective-permute-start | bytes 1534472 | tf_op jit(solution)/shard_map/while/body/eval_jaxpr/ppermute | solution.py:14
  60.0 7.6 %collective-permute-done.1 = s32[48,24]{1,0:T(8,128)S(1)} collective-permute-done((s32[48,24]{1,0:T(8,128)S(1)}, s32[48,24]{1,0:T(8,128)S(1)}, u32[]{:S(2)}, u32[]{:S(2)}) %collective-permute-start.1) | collective-permute-done | bytes 4640 | tf_op jit(solution)/shard_map/while/body/eval_jaxpr/ppermute | solution.py:14
  73.7 7.6 %collective-permute-done.1 = s32[48,24]{1,0:T(8,128)S(1)} collective-permute-done((s32[48,24]{1,0:T(8,128)S(1)}, s32[48,24]{1,0:T(8,128)S(1)}, u32[]{:S(2)}, u32[]{:S(2)}) %collective-permute-start.1) | collective-permute-done | bytes 4640 | tf_op jit(solution)/shard_map/while/body/eval_jaxpr/ppermute | solution.py:14
  82.8 4.6 %collective-permute-start = (bf16[48,24,222]{2,1,0:T(8,128)(2,1)S(1)}, bf16[48,24,222]{2,1,0:T(8,128)(2,1)S(1)}, u32[]{:S(2)}, u32[]{:S(2)}) collective-permute-start(bf16[48,24,222]{2,1,0:T(8,128)(2,1)S(1)} %get-tuple-element.302), channel_id=1, source_target_pairs={{0,30},{2,0},{4,2},{6,4},{8,6},{10,8},{12,10},{14,12},{16,14},{18,... | collective-permute-start | bytes 1534472 | tf_op jit(solution)/shard_map/while/body/eval_jaxpr/ppermute | solution.py:14
  87.5 7.6 %collective-permute-done.1 = s32[48,24]{1,0:T(8,128)S(1)} collective-permute-done((s32[48,24]{1,0:T(8,128)S(1)}, s32[48,24]{1,0:T(8,128)S(1)}, u32[]{:S(2)}, u32[]{:S(2)}) %collective-permute-start.1) | collective-permute-done | bytes 4640 | tf_op jit(solution)/shard_map/while/body/eval_jaxpr/ppermute | solution.py:14
  101.3 7.6 %collective-permute-done.1 = s32[48,24]{1,0:T(8,128)S(1)} collective-permute-done((s32[48,24]{1,0:T(8,128)S(1)}, s32[48,24]{1,0:T(8,128)S(1)}, u32[]{:S(2)}, u32[]{:S(2)}) %collective-permute-start.1) | collective-permute-done | bytes 4640 | tf_op jit(solution)/shard_map/while/body/eval_jaxpr/ppermute | solution.py:14
  115.1 7.6 %collective-permute-done.1 = s32[48,24]{1,0:T(8,128)S(1)} collective-permute-done((s32[48,24]{1,0:T(8,128)S(1)}, s32[48,24]{1,0:T(8,128)S(1)}, u32[]{:S(2)}, u32[]{:S(2)}) %collective-permute-start.1) | collective-permute-done | bytes 4640 | tf_op jit(solution)/shard_map/while/body/eval_jaxpr/ppermute | solution.py:14
  124.2 4.6 %collective-permute-start = (bf16[48,24,222]{2,1,0:T(8,128)(2,1)S(1)}, bf16[48,24,222]{2,1,0:T(8,128)(2,1)S(1)}, u32[]{:S(2)}, u32[]{:S(2)}) collective-permute-start(bf16[48,24,222]{2,1,0:T(8,128)(2,1)S(1)} %get-tuple-element.302), channel_id=1, source_target_pairs={{0,30},{2,0},{4,2},{6,4},{8,6},{10,8},{12,10},{14,12},{16,14},{18,... | collective-permute-start | bytes 1534472 | tf_op jit(solution)/shard_map/while/body/eval_jaxpr/ppermute | solution.py:14
  128.8 7.6 %collective-permute-done.1 = s32[48,24]{1,0:T(8,128)S(1)} collective-permute-done((s32[48,24]{1,0:T(8,128)S(1)}, s32[48,24]{1,0:T(8,128)S(1)}, u32[]{:S(2)}, u32[]{:S(2)}) %collective-permute-start.1) | collective-permute-done | bytes 4640 | tf_op jit(solution)/shard_map/while/body/eval_jaxpr/ppermute | solution.py:14
  142.6 7.6 %collective-permute-done.1 = s32[48,24]{1,0:T(8,128)S(1)} collective-permute-done((s32[48,24]{1,0:T(8,128)S(1)}, s32[48,24]{1,0:T(8,128)S(1)}, u32[]{:S(2)}, u32[]{:S(2)}) %collective-permute-start.1) | collective-permute-done | bytes 4640 | tf_op jit(solution)/shard_map/while/body/eval_jaxpr/ppermute | solution.py:14
  156.3 7.6 %collective-permute-done.1 = s32[48,24]{1,0:T(8,128)S(1)} collective-permute-done((s32[48,24]{1,0:T(8,128)S(1)}, s32[48,24]{1,0:T(8,128)S(1)}, u32[]{:S(2)}, u32[]{:S(2)}) %collective-permute-start.1) | collective-permute-done | bytes 4640 | tf_op jit(solution)/shard_map/while/body/eval_jaxpr/ppermute | solution.py:14
  170.0 7.6 %collective-permute-done.1 = s32[48,24]{1,0:T(8,128)S(1)} collective-permute-done((s32[48,24]{1,0:T(8,128)S(1)}, s32[48,24]{1,0:T(8,128)S(1)}, u32[]{:S(2)}, u32[]{:S(2)}) %collective-permute-start.1) | collective-permute-done | bytes 4640 | tf_op jit(solution)/shard_map/while/body/eval_jaxpr/ppermute | solution.py:14
  183.6 7.6 %collective-permute-done.1 = s32[48,24]{1,0:T(8,128)S(1)} collective-permute-done((s32[48,24]{1,0:T(8,128)S(1)}, s32[48,24]{1,0:T(8,128)S(1)}, u32[]{:S(2)}, u32[]{:S(2)}) %collective-permute-start.1) | collective-permute-done | bytes 4640 | tf_op jit(solution)/shard_map/while/body/eval_jaxpr/ppermute | solution.py:14
  197.3 7.6 %collective-permute-done.1 = s32[48,24]{1,0:T(8,128)S(1)} collective-permute-done((s32[48,24]{1,0:T(8,128)S(1)}, s32[48,24]{1,0:T(8,128)S(1)}, u32[]{:S(2)}, u32[]{:S(2)}) %collective-permute-start.1) | collective-permute-done | bytes 4640 | tf_op jit(solution)/shard_map/while/body/eval_jaxpr/ppermute | solution.py:14
  206.3 39.3 %while.34 = (s32[]{:T(128)}, f32[8,24,222]{2,1,0:T(8,128)S(1)}, f32[8,24,222]{2,1,0:T(8,128)}, f32[8,24,222]{2,1,0:T(8,128)}, s32[8]{0:T(128)S(1)}, /*index=5*/s...) while((s32[]{:T(128)}, f32[8,24,222]{2,1,0:T(8,128)S(1)}, ...), condition=%wide.region_6.7_spmd, body=%wide.region_2.6_spmd.sunk | while | flops 2288021 | bytes 1758447 | solution.py:63
  247.8 10.9 %reduce-scatter.4.cloned.1.call-done = f32[4,24,222]{2,1,0:T(8,128)} async-done(((f32[8,24,222]{2,1,0:T(8,128)}), f32[4,24,222]{2,1,0:T(8,128)}) %reduce-scatter.4.cloned.1.call-update) | async-done | bytes 85264 | tf_op jit(solution)/shard_map/reduce_scatter | solution.py:65
  258.7 13.2 %reduce-scatter.6.cloned.1.call-done = f32[4,24,222]{2,1,0:T(8,128)} async-done(((f32[8,24,222]{2,1,0:T(8,128)}), f32[4,24,222]{2,1,0:T(8,128)}) %reduce-scatter.6.cloned.1.call-update) | async-done | bytes 85264 | tf_op jit(solution)/shard_map/reduce_scatter | solution.py:66
  271.9 13.3 %reduce-scatter.8.cloned.1.call-done = f32[4,24,222]{2,1,0:T(8,128)} async-done(((f32[8,24,222]{2,1,0:T(8,128)}), f32[4,24,222]{2,1,0:T(8,128)}) %reduce-scatter.8.cloned.1.call-update) | async-done | bytes 85264 | tf_op jit(solution)/shard_map/reduce_scatter | solution.py:67
  (153 shorter events, 97.2 us)
Async XLA Ops:
  6.5 252.2 %reduce-scatter.4.cloned.1.call-start = ((), (), s32[]{:S(2)}) async-start(), calls=%async_computation.3 | async-start | bytes 294912 | tf_op jit(solution)/shard_map/reduce_scatter | solution.py:65
  13.2 13.6 %collective-permute-start = (bf16[48,24,222]{2,1,0:T(8,128)(2,1)S(1)}, bf16[48,24,222]{2,1,0:T(8,128)(2,1)S(1)}, u32[]{:S(2)}, u32[]{:S(2)}) collective-permute-start(bf16[48,24,222]{2,1,0:T(8,128)(2,1)S(1)} %get-tuple-element.302), channel_id=1, source_target_pairs={{0,30},{2,0},{4,2},{6,4},{8,6},{10,8},{12,10},{14,12},{16,14},{18,... | collective-permute-start | bytes 1534472 | tf_op jit(solution)/shard_map/while/body/eval_jaxpr/ppermute | solution.py:14
  18.6 7.7 %collective-permute-start.1 = (s32[48,24]{1,0:T(8,128)S(1)}, s32[48,24]{1,0:T(8,128)S(1)}, u32[]{:S(2)}, u32[]{:S(2)}) collective-permute-start(s32[48,24]{1,0:T(8,128)S(1)} %get-tuple-element.303), channel_id=1, source_target_pairs={{0,30},{2,0},{4,2},{6,4},{8,6},{10,8},{12,10},{14,12},{16,14},{18,... | collective-permute-start | bytes 13832 | tf_op jit(solution)/shard_map/while/body/eval_jaxpr/ppermute | solution.py:14
  27.8 12.8 %collective-permute-start = (bf16[48,24,222]{2,1,0:T(8,128)(2,1)S(1)}, bf16[48,24,222]{2,1,0:T(8,128)(2,1)S(1)}, u32[]{:S(2)}, u32[]{:S(2)}) collective-permute-start(bf16[48,24,222]{2,1,0:T(8,128)(2,1)S(1)} %get-tuple-element.302), channel_id=1, source_target_pairs={{0,30},{2,0},{4,2},{6,4},{8,6},{10,8},{12,10},{14,12},{16,14},{18,... | collective-permute-start | bytes 1534472 | tf_op jit(solution)/shard_map/while/body/eval_jaxpr/ppermute | solution.py:14
  32.4 7.7 %collective-permute-start.1 = (s32[48,24]{1,0:T(8,128)S(1)}, s32[48,24]{1,0:T(8,128)S(1)}, u32[]{:S(2)}, u32[]{:S(2)}) collective-permute-start(s32[48,24]{1,0:T(8,128)S(1)} %get-tuple-element.303), channel_id=1, source_target_pairs={{0,30},{2,0},{4,2},{6,4},{8,6},{10,8},{12,10},{14,12},{16,14},{18,... | collective-permute-start | bytes 13832 | tf_op jit(solution)/shard_map/while/body/eval_jaxpr/ppermute | solution.py:14
  41.6 12.8 %collective-permute-start = (bf16[48,24,222]{2,1,0:T(8,128)(2,1)S(1)}, bf16[48,24,222]{2,1,0:T(8,128)(2,1)S(1)}, u32[]{:S(2)}, u32[]{:S(2)}) collective-permute-start(bf16[48,24,222]{2,1,0:T(8,128)(2,1)S(1)} %get-tuple-element.302), channel_id=1, source_target_pairs={{0,30},{2,0},{4,2},{6,4},{8,6},{10,8},{12,10},{14,12},{16,14},{18,... | collective-permute-start | bytes 1534472 | tf_op jit(solution)/shard_map/while/body/eval_jaxpr/ppermute | solution.py:14
  46.2 7.7 %collective-permute-start.1 = (s32[48,24]{1,0:T(8,128)S(1)}, s32[48,24]{1,0:T(8,128)S(1)}, u32[]{:S(2)}, u32[]{:S(2)}) collective-permute-start(s32[48,24]{1,0:T(8,128)S(1)} %get-tuple-element.303), channel_id=1, source_target_pairs={{0,30},{2,0},{4,2},{6,4},{8,6},{10,8},{12,10},{14,12},{16,14},{18,... | collective-permute-start | bytes 13832 | tf_op jit(solution)/shard_map/while/body/eval_jaxpr/ppermute | solution.py:14
  55.3 12.8 %collective-permute-start = (bf16[48,24,222]{2,1,0:T(8,128)(2,1)S(1)}, bf16[48,24,222]{2,1,0:T(8,128)(2,1)S(1)}, u32[]{:S(2)}, u32[]{:S(2)}) collective-permute-start(bf16[48,24,222]{2,1,0:T(8,128)(2,1)S(1)} %get-tuple-element.302), channel_id=1, source_target_pairs={{0,30},{2,0},{4,2},{6,4},{8,6},{10,8},{12,10},{14,12},{16,14},{18,... | collective-permute-start | bytes 1534472 | tf_op jit(solution)/shard_map/while/body/eval_jaxpr/ppermute | solution.py:14
  59.9 7.7 %collective-permute-start.1 = (s32[48,24]{1,0:T(8,128)S(1)}, s32[48,24]{1,0:T(8,128)S(1)}, u32[]{:S(2)}, u32[]{:S(2)}) collective-permute-start(s32[48,24]{1,0:T(8,128)S(1)} %get-tuple-element.303), channel_id=1, source_target_pairs={{0,30},{2,0},{4,2},{6,4},{8,6},{10,8},{12,10},{14,12},{16,14},{18,... | collective-permute-start | bytes 13832 | tf_op jit(solution)/shard_map/while/body/eval_jaxpr/ppermute | solution.py:14
  69.1 12.8 %collective-permute-start = (bf16[48,24,222]{2,1,0:T(8,128)(2,1)S(1)}, bf16[48,24,222]{2,1,0:T(8,128)(2,1)S(1)}, u32[]{:S(2)}, u32[]{:S(2)}) collective-permute-start(bf16[48,24,222]{2,1,0:T(8,128)(2,1)S(1)} %get-tuple-element.302), channel_id=1, source_target_pairs={{0,30},{2,0},{4,2},{6,4},{8,6},{10,8},{12,10},{14,12},{16,14},{18,... | collective-permute-start | bytes 1534472 | tf_op jit(solution)/shard_map/while/body/eval_jaxpr/ppermute | solution.py:14
  73.7 7.7 %collective-permute-start.1 = (s32[48,24]{1,0:T(8,128)S(1)}, s32[48,24]{1,0:T(8,128)S(1)}, u32[]{:S(2)}, u32[]{:S(2)}) collective-permute-start(s32[48,24]{1,0:T(8,128)S(1)} %get-tuple-element.303), channel_id=1, source_target_pairs={{0,30},{2,0},{4,2},{6,4},{8,6},{10,8},{12,10},{14,12},{16,14},{18,... | collective-permute-start | bytes 13832 | tf_op jit(solution)/shard_map/while/body/eval_jaxpr/ppermute | solution.py:14
  82.8 12.8 %collective-permute-start = (bf16[48,24,222]{2,1,0:T(8,128)(2,1)S(1)}, bf16[48,24,222]{2,1,0:T(8,128)(2,1)S(1)}, u32[]{:S(2)}, u32[]{:S(2)}) collective-permute-start(bf16[48,24,222]{2,1,0:T(8,128)(2,1)S(1)} %get-tuple-element.302), channel_id=1, source_target_pairs={{0,30},{2,0},{4,2},{6,4},{8,6},{10,8},{12,10},{14,12},{16,14},{18,... | collective-permute-start | bytes 1534472 | tf_op jit(solution)/shard_map/while/body/eval_jaxpr/ppermute | solution.py:14
  87.4 7.7 %collective-permute-start.1 = (s32[48,24]{1,0:T(8,128)S(1)}, s32[48,24]{1,0:T(8,128)S(1)}, u32[]{:S(2)}, u32[]{:S(2)}) collective-permute-start(s32[48,24]{1,0:T(8,128)S(1)} %get-tuple-element.303), channel_id=1, source_target_pairs={{0,30},{2,0},{4,2},{6,4},{8,6},{10,8},{12,10},{14,12},{16,14},{18,... | collective-permute-start | bytes 13832 | tf_op jit(solution)/shard_map/while/body/eval_jaxpr/ppermute | solution.py:14
  96.6 12.8 %collective-permute-start = (bf16[48,24,222]{2,1,0:T(8,128)(2,1)S(1)}, bf16[48,24,222]{2,1,0:T(8,128)(2,1)S(1)}, u32[]{:S(2)}, u32[]{:S(2)}) collective-permute-start(bf16[48,24,222]{2,1,0:T(8,128)(2,1)S(1)} %get-tuple-element.302), channel_id=1, source_target_pairs={{0,30},{2,0},{4,2},{6,4},{8,6},{10,8},{12,10},{14,12},{16,14},{18,... | collective-permute-start | bytes 1534472 | tf_op jit(solution)/shard_map/while/body/eval_jaxpr/ppermute | solution.py:14
  110.4 12.8 %collective-permute-start = (bf16[48,24,222]{2,1,0:T(8,128)(2,1)S(1)}, bf16[48,24,222]{2,1,0:T(8,128)(2,1)S(1)}, u32[]{:S(2)}, u32[]{:S(2)}) collective-permute-start(bf16[48,24,222]{2,1,0:T(8,128)(2,1)S(1)} %get-tuple-element.302), channel_id=1, source_target_pairs={{0,30},{2,0},{4,2},{6,4},{8,6},{10,8},{12,10},{14,12},{16,14},{18,... | collective-permute-start | bytes 1534472 | tf_op jit(solution)/shard_map/while/body/eval_jaxpr/ppermute | solution.py:14
  124.2 12.8 %collective-permute-start = (bf16[48,24,222]{2,1,0:T(8,128)(2,1)S(1)}, bf16[48,24,222]{2,1,0:T(8,128)(2,1)S(1)}, u32[]{:S(2)}, u32[]{:S(2)}) collective-permute-start(bf16[48,24,222]{2,1,0:T(8,128)(2,1)S(1)} %get-tuple-element.302), channel_id=1, source_target_pairs={{0,30},{2,0},{4,2},{6,4},{8,6},{10,8},{12,10},{14,12},{16,14},{18,... | collective-permute-start | bytes 1534472 | tf_op jit(solution)/shard_map/while/body/eval_jaxpr/ppermute | solution.py:14
  137.9 12.8 %collective-permute-start = (bf16[48,24,222]{2,1,0:T(8,128)(2,1)S(1)}, bf16[48,24,222]{2,1,0:T(8,128)(2,1)S(1)}, u32[]{:S(2)}, u32[]{:S(2)}) collective-permute-start(bf16[48,24,222]{2,1,0:T(8,128)(2,1)S(1)} %get-tuple-element.302), channel_id=1, source_target_pairs={{0,30},{2,0},{4,2},{6,4},{8,6},{10,8},{12,10},{14,12},{16,14},{18,... | collective-permute-start | bytes 1534472 | tf_op jit(solution)/shard_map/while/body/eval_jaxpr/ppermute | solution.py:14
  151.7 12.7 %collective-permute-start = (bf16[48,24,222]{2,1,0:T(8,128)(2,1)S(1)}, bf16[48,24,222]{2,1,0:T(8,128)(2,1)S(1)}, u32[]{:S(2)}, u32[]{:S(2)}) collective-permute-start(bf16[48,24,222]{2,1,0:T(8,128)(2,1)S(1)} %get-tuple-element.302), channel_id=1, source_target_pairs={{0,30},{2,0},{4,2},{6,4},{8,6},{10,8},{12,10},{14,12},{16,14},{18,... | collective-permute-start | bytes 1534472 | tf_op jit(solution)/shard_map/while/body/eval_jaxpr/ppermute | solution.py:14
  165.3 12.7 %collective-permute-start = (bf16[48,24,222]{2,1,0:T(8,128)(2,1)S(1)}, bf16[48,24,222]{2,1,0:T(8,128)(2,1)S(1)}, u32[]{:S(2)}, u32[]{:S(2)}) collective-permute-start(bf16[48,24,222]{2,1,0:T(8,128)(2,1)S(1)} %get-tuple-element.302), channel_id=1, source_target_pairs={{0,30},{2,0},{4,2},{6,4},{8,6},{10,8},{12,10},{14,12},{16,14},{18,... | collective-permute-start | bytes 1534472 | tf_op jit(solution)/shard_map/while/body/eval_jaxpr/ppermute | solution.py:14
  169.9 7.7 %collective-permute-start.1 = (s32[48,24]{1,0:T(8,128)S(1)}, s32[48,24]{1,0:T(8,128)S(1)}, u32[]{:S(2)}, u32[]{:S(2)}) collective-permute-start(s32[48,24]{1,0:T(8,128)S(1)} %get-tuple-element.303), channel_id=1, source_target_pairs={{0,30},{2,0},{4,2},{6,4},{8,6},{10,8},{12,10},{14,12},{16,14},{18,... | collective-permute-start | bytes 13832 | tf_op jit(solution)/shard_map/while/body/eval_jaxpr/ppermute | solution.py:14
  179.0 12.7 %collective-permute-start = (bf16[48,24,222]{2,1,0:T(8,128)(2,1)S(1)}, bf16[48,24,222]{2,1,0:T(8,128)(2,1)S(1)}, u32[]{:S(2)}, u32[]{:S(2)}) collective-permute-start(bf16[48,24,222]{2,1,0:T(8,128)(2,1)S(1)} %get-tuple-element.302), channel_id=1, source_target_pairs={{0,30},{2,0},{4,2},{6,4},{8,6},{10,8},{12,10},{14,12},{16,14},{18,... | collective-permute-start | bytes 1534472 | tf_op jit(solution)/shard_map/while/body/eval_jaxpr/ppermute | solution.py:14
  192.6 12.7 %collective-permute-start = (bf16[48,24,222]{2,1,0:T(8,128)(2,1)S(1)}, bf16[48,24,222]{2,1,0:T(8,128)(2,1)S(1)}, u32[]{:S(2)}, u32[]{:S(2)}) collective-permute-start(bf16[48,24,222]{2,1,0:T(8,128)(2,1)S(1)} %get-tuple-element.302), channel_id=1, source_target_pairs={{0,30},{2,0},{4,2},{6,4},{8,6},{10,8},{12,10},{14,12},{16,14},{18,... | collective-permute-start | bytes 1534472 | tf_op jit(solution)/shard_map/while/body/eval_jaxpr/ppermute | solution.py:14
  246.3 25.6 %reduce-scatter.6.cloned.1.call-start = ((), (), s32[]{:S(2)}) async-start(), calls=%async_computation.4 | async-start | bytes 294912 | tf_op jit(solution)/shard_map/reduce_scatter | solution.py:66
  247.0 38.2 %reduce-scatter.8.cloned.1.call-start = ((), (), s32[]{:S(2)}) async-start(), calls=%async_computation.5 | async-start | bytes 294912 | tf_op jit(solution)/shard_map/reduce_scatter | solution.py:67
  (9 other events, 247.5 us)
Sparse Core Ops, SparseCore 0:
  246.4 12.2 reduce-scatter.3
  260.9 10.9 reduce-scatter.5
  274.2 10.9 reduce-scatter.7
where the time goes:
time: 294 us; the launch traced here: 293 us
  waiting for transfers between devices  145 us (49%)
  starting transfers between devices  66.5 us (23%)
  local copies, waits for them, and re-layouts  35.4 us (12%)
  other arithmetic  17.7 us (6%)
  loops' own time  15.5 us (5%)
  between operations  13.1 us (4%)
    ppermute x28, waiting for transfers between devices, from_behind(): lax.ppermute(value, axis, [(i, (i + by) % count) for i in range(count)])  106 us
    ppermute x28, starting transfers between devices, from_behind(): lax.ppermute(value, axis, [(i, (i + by) % count) for i in range(count)])  66.5 us
    another operation x1, loops' own time, local(): lax.map(lag_sums, eastward_offsets)  15.1 us
    reduce_sum x8, other arithmetic, lag_sums(): var_true = jnp.sum(couple_factor * frame_segment * frame_segment, axis=0)  13.7 us
    reduce_scatter x1, waiting for transfers between devices, local(): lax.psum_scatter(var_true, 'lat', scatter_dimension=0, tiled=True)  13.3 us
    reduce_scatter x1, waiting for transfers between devices, local(): lax.psum_scatter(prediction_spread, 'lat', scatter_dimension=0, tiled=True)  13.2 us
    dynamic_update_slice x14, local copies, waits for them, and re-layouts, advance(): lax.dynamic_update_slice_in_dim(buffer_true, slab_true, place, 1)  12.7 us
    reduce_scatter x1, waiting for transfers between devices, local(): lax.psum_scatter(joint_moment, 'lat', scatter_dimension=0, tiled=True)  10.9 us
  transfers between devices with their start and end apart: 31, of which 17 were waited for; matrix products, arithmetic and copies ran while one was open for 2% of the time, Pallas kernels for 0%

commit v1 on v0

--- a/solution.py
+++ b/solution.py
@@ -1,12 +1,238 @@
+import functools
+import math
+
 import jax
 import jax.numpy as jnp
 from jax import lax
+from jax.experimental import pallas as pl
+from jax.experimental.pallas import tpu as pltpu
 from jax.sharding import PartitionSpec as P
 
+MESH = pl.DeviceIdType.MESH
+LANES = 128
+SLOTS = 8
+regular_term = 0.001
+
+
+def exchange_kernel(n_lat, n_lon, src, dst, send_sem, recv_sem, own_sem):
+    n = n_lat * n_lon
+    me = lax.axis_index("lat") * n_lon + lax.axis_index("lon")
+
+    def place(g):
+        return {"lat": g // n_lon, "lon": g % n_lon}
+
+    barrier = pltpu.get_barrier_semaphore()
+
+    def greet(o, _):
+        pl.semaphore_signal(barrier, inc=1, device_id=place((me + o) % n), device_id_type=MESH)
+        return 0
+
+    lax.fori_loop(1, n, greet, 0)
+    own = pltpu.make_async_copy(src.at[me], dst.at[me], own_sem)
+    own.start()
+    pl.semaphore_wait(barrier, n - 1)
+
+    def outgoing(o):
+        there = (me + o) % n
+        return pltpu.make_async_remote_copy(
+            src_ref=src.at[there],
+            dst_ref=dst.at[me],
+            send_sem=send_sem.at[o],
+            recv_sem=recv_sem.at[o],
+            device_id=place(there),
+            device_id_type=MESH,
+        )
+
+    def start(o, _):
+        outgoing(o).start()
+        return 0
+
+    def finish(o, _):
+        outgoing(o).wait()
+        return 0
+
+    lax.fori_loop(1, n, start, 0)
+    lax.fori_loop(1, n, finish, 0)
+    own.wait()
+
+
+def exchange(value, n_lat, n_lon, collective_id):
+    n = n_lat * n_lon
+    return pl.pallas_call(
+        functools.partial(exchange_kernel, n_lat, n_lon),
+        out_shape=jax.ShapeDtypeStruct(value.shape, value.dtype),
+        in_specs=[pl.BlockSpec(memory_space=pltpu.VMEM)],
+        out_specs=pl.BlockSpec(memory_space=pltpu.VMEM),
+        scratch_shapes=[
+            pltpu.SemaphoreType.DMA((n,)),
+            pltpu.SemaphoreType.DMA((n,)),
+            pltpu.SemaphoreType.DMA,
+        ],
+        compiler_params=pltpu.CompilerParams(
+            collective_id=collective_id, has_side_effects=True, vmem_limit_bytes=40 * 2**20
+        ),
+    )(value)
+
+
+def lag_kernel(sizes, offsets, weights, got, out, fore_w, fore_ww, weight, truth):
+    n_lat, n_lon, rows, cols, lags = sizes
+    tiles = n_lon * cols // LANES
+    group = math.lcm(cols, LANES) // cols
+    blocks = rows // group
+    width = group * cols
+    per_owner = lags // n_lat
+    flag = SLOTS - 1
+
+    def unpack(step, _):
+        half, block = step // blocks, step % blocks
+        base = half * rows + block * group
+        for d in range(n_lon):
+            chunk = got[half * n_lon + d, :, pl.ds(pl.multiple_of(block * width, LANES), width)]
+            chunk = chunk.astype(jnp.float32)
+            for i in range(group):
+                piece = chunk[:, i * cols : (i + 1) * cols]
+                fore_w[base + i, :, d * cols : (d + 1) * cols] = piece[:SLOTS]
+                truth[base + i, :, d * cols : (d + 1) * cols] = piece[SLOTS:]
+        return 0
+
+    lax.fori_loop(0, n_lat * blocks, unpack, 0)
+
+    def prepare(i, _):
+        w = weights[i]
+        for m in range(tiles):
+            at = pl.ds(m * LANES, LANES)
+            fore = fore_w[i, :, at]
+            usable = w * jnp.broadcast_to(fore[flag:, :], fore.shape)
+            weighted = usable * fore
+            weight[i, :, at] = usable
+            fore_w[i, :, at] = weighted
+            fore_ww[i, :, at] = weighted * fore
+            true = truth[i, :, at]
+            true = true * jnp.broadcast_to(true[flag:, :], true.shape)
+            truth[i, :, at] = true
+            if m < tiles - 1:
+                truth[i, :, pl.ds((tiles + m) * LANES, LANES)] = true
+        return 0
+
+    lax.fori_loop(0, n_lat * rows, prepare, 0)
+
+    lane = lax.broadcasted_iota(jnp.int32, (SLOTS, LANES), 1)
+    zero = jnp.zeros((SLOTS, LANES), jnp.float32)
+    for k in range(lags):
+        first = offsets[k] // LANES
+        turn = offsets[k] % LANES
+        back = (LANES - turn) % LANES
+        stay = lane < LANES - turn
+
+        def row(i, totals):
+            turned = [
+                pltpu.roll(
+                    truth[i, :, pl.ds(pl.multiple_of((first + m) * LANES, LANES), LANES)], back, 1
+                )
+                for m in range(tiles)
+            ]
+            result = []
+            for m in range(tiles):
+                at = pl.ds(m * LANES, LANES)
+                true = jnp.where(stay, turned[m], turned[(m + 1) % tiles])
+                seen = jnp.broadcast_to(true[flag:, :], true.shape)
+                cov, var_fore, var_true = totals[m]
+                result.append(
+                    (
+                        cov + fore_w[i, :, at] * true,
+                        var_fore + fore_ww[i, :, at] * seen,
+                        var_true + weight[i, :, at] * (true * true),
+                    )
+                )
+            return tuple(result)
+
+        totals = lax.fori_loop(
+            0, n_lat * rows, row, tuple((zero, zero, zero) for _ in range(tiles)), unroll=4
+        )
+        found = jnp.concatenate(
+            [
+                cov / jnp.sqrt((var_fore + regular_term) * (var_true + regular_term))
+                for cov, var_fore, var_true in totals
+            ],
+            axis=1,
+        )
+        owner, at = k // per_owner, k % per_owner
+        for d in range(n_lon):
+            out[owner * n_lon + d, :, at * cols : (at + 1) * cols] = found[
+                :, d * cols : (d + 1) * cols
+            ]
+
+
+def by_channel(n_lat, n_lon, prediction, observed_state, mean_state, usable_point_flags, offsets):
+    rows, cols, channels = prediction.shape
+    lags = offsets.shape[0]
+    n = n_lat * n_lon
+    share = -(-channels // n)
+    points = rows * cols
+    total_rows, total_cols = rows * n_lat, cols * n_lon
+    mean = mean_state.astype(jnp.float32)
+    fore = (prediction.astype(jnp.float32) - mean).astype(jnp.bfloat16).reshape(points, channels)
+    true = (observed_state.astype(jnp.float32) - mean).astype(jnp.bfloat16).reshape(points, channels)
+
+    index = jnp.arange(n * 2 * SLOTS, dtype=jnp.int32)
+    owner, slot = index // (2 * SLOTS), index % (2 * SLOTS)
+    place = slot % SLOTS
+    wanted = jnp.where(place < share, owner * share + place, -1)[:, None]
+    hit = wanted == jnp.arange(channels, dtype=jnp.int32)[None, :]
+    pick_fore = (hit & (slot < SLOTS)[:, None]).astype(jnp.bfloat16)
+    pick_true = (hit & (slot >= SLOTS)[:, None]).astype(jnp.bfloat16)
+    turn = functools.partial(
+        lax.dot_general,
+        dimension_numbers=(((1,), (1,)), ((), ())),
+        preferred_element_type=jnp.float32,
+    )
+    packed = turn(pick_fore, fore) + turn(pick_true, true)
+    flags = usable_point_flags.astype(jnp.float32).reshape(1, points)
+    packed = jnp.where((place == SLOTS - 1)[:, None], flags, packed).astype(jnp.bfloat16)
+
+    got = exchange(packed.reshape(n, 2 * SLOTS, points), n_lat, n_lon, 0)
+
+    row_index = jnp.arange(total_rows, dtype=jnp.int32).astype(jnp.float32)
+    weights = jnp.cos(jnp.pi * ((row_index + 0.5) / total_rows - 0.5))
+    tiles = total_cols // LANES
+    held = (total_rows, SLOTS, total_cols)
+    found = pl.pallas_call(
+        functools.partial(lag_kernel, (n_lat, n_lon, rows, cols, lags)),
+        out_shape=jax.ShapeDtypeStruct((n, SLOTS, LANES), jnp.float32),
+        in_specs=[
+            pl.BlockSpec(memory_space=pltpu.SMEM),
+            pl.BlockSpec(memory_space=pltpu.SMEM),
+            pl.BlockSpec(memory_space=pltpu.VMEM),
+        ],
+        out_specs=pl.BlockSpec(memory_space=pltpu.VMEM),
+        scratch_shapes=[
+            pltpu.VMEM(held, jnp.float32),
+            pltpu.VMEM(held, jnp.float32),
+            pltpu.VMEM(held, jnp.float32),
+            pltpu.VMEM((total_rows, SLOTS, (2 * tiles - 1) * LANES), jnp.float32),
+        ],
+        compiler_params=pltpu.CompilerParams(vmem_limit_bytes=40 * 2**20),
+    )(offsets, weights, got)
+
+    back = exchange(found, n_lat, n_lon, 1)
+    mine = lags // n_lat
+    back = back[:, :share, : mine * cols].reshape(n * share, mine, cols)[:channels]
+    return back.transpose(1, 2, 0)
+
+
+def fits(n_lat, n_lon, rows, cols, channels, lags):
+    n = n_lat * n_lon
+    group = math.lcm(cols, LANES) // cols
+    return (
+        -(-channels // n) < SLOTS
+        and n <= channels
+        and rows % group == 0
+        and (cols * n_lon) % LANES == 0
+        and lags // n_lat * cols <= LANES
+    )
+
+
 REACH = 14
-
-
-regular_term = 0.001
 
 
 def from_behind(value, axis, by):
@@ -14,7 +240,7 @@
     return lax.ppermute(value, axis, [(i, (i + by) % count) for i in range(count)])
 
 
-def local(prediction, observed_state, mean_state, usable_point_flags, eastward_offsets):
+def ring(prediction, observed_state, mean_state, usable_point_flags, eastward_offsets):
     meridian_extent, parallel_extent, field_total = prediction.shape
     total_rows = meridian_extent * lax.axis_size("lat")
     row_index = (
@@ -70,6 +296,7 @@
 
 
 def solution(mesh):
+    n_lat, n_lon = mesh.shape["lat"], mesh.shape["lon"]
     placed = (
         P("lat", "lon", None),
         P("lat", "lon", None),
@@ -77,6 +304,12 @@
         P("lat", "lon"),
         P(),
     )
+
+    def local(*args):
+        if fits(n_lat, n_lon, *args[0].shape, args[4].shape[0]):
+            return by_channel(n_lat, n_lon, *args)
+        return ring(*args)
+
     return jax.shard_map(
         local, mesh=mesh, in_specs=placed, out_specs=P("lat", "lon", None), check_vma=False
     )

time: 294 us -> 68.9 us (0.23)
  waiting for transfers between devices: 145 us -> 0 us
  starting transfers between devices: 66.5 us -> 0 us
  Pallas kernels: 0 us -> 64.1 us
  local copies, waits for them, and re-layouts: 35.4 us -> 1.39 us
  other arithmetic: 17.7 us -> 1.77 us
  loops' own time: 15.5 us -> 0 us
  between operations: 13.1 us -> 0.1 us
    ppermute x28 -> x0, waiting for transfers between devices: 106 us -> none  [from_behind(): lax.ppermute(value, axis, [(i, (i + by) % count) for i in range(count)])]
    ppermute x28 -> x0, starting transfers between devices: 66.5 us -> none  [from_behind(): lax.ppermute(value, axis, [(i, (i + by) % count) for i in range(count)])]
    pallas_call x0 -> x3, Pallas kernels: none -> 64.1 us  [the longest x2 43.2 us: exchange(): pl.pallas_call(functools.partial(exchange_kernel, n_lat, n_lon), out_shap...]
    reduce_scatter x3 -> x0, waiting for transfers between devices: 37.4 us -> none  [the longest x1 13.3 us: local(): lax.psum_scatter(var_true, 'lat', scatter_dimension=0, tiled=True)]
    dynamic_update_slice x46 -> x0, local copies, waits for them, and re-layouts: 28.6 us -> none  [the longest x14 12.7 us: advance(): lax.dynamic_update_slice_in_dim(buffer_true, slab_true, place, 1)]
    another operation x2 -> x0, loops' own time: 15.5 us -> none  [the longest x1 15.1 us: local(): lax.map(lag_sums, eastward_offsets)]
    reduce_sum x8 -> x0, other arithmetic: 13.7 us -> none  [lag_sums(): var_true = jnp.sum(couple_factor * frame_segment * frame_segment, axis=0)]
    dynamic_slice x8 -> x0, local copies, waits for them, and re-layouts: 4.76 us -> none  [local(): lax.map(lag_sums, eastward_offsets)]
  transfers between devices with their start and end apart: 31 -> 0, of which waited for: 17 -> 0; matrix products, arithmetic and copies ran while one was open for 2% -> 0% of each run, Pallas kernels for 0% -> 0%
where the time goes in v1:
time: 68.9 us; the launch traced here: 68.6 us
  Pallas kernels  64.1 us (93%)
  other arithmetic  1.77 us (3%)
  local copies, waits for them, and re-layouts  1.39 us (2%)
  matrix products  1.2 us (2%)
    pallas_call x2, Pallas kernels, exchange(): pl.pallas_call(functools.partial(exchange_kernel, n_lat, n_lon), out_shap...  43.2 us
    pallas_call x1, Pallas kernels, by_channel(): pl.pallas_call(functools.partial(lag_kernel, (n_lat, n_lon, rows, cols, l...  21 us
    convert_element_type x1, other arithmetic, by_channel(): (observed_state.astype(jnp.float32) - mean).astype(jnp.bfloat16)  1.7 us

profile of v1, /device:TPU:0, one launch (start us, length us, event | category | flops | bytes accessed | tf_op | source)
XLA Modules:
  0.0 68.6 jit_solution(3927139766137746827)
XLA Ops:
  0.0 1.7 %fusion.3 = (bf16[48,24,222]{2,1,0:T(8,128)(2,1)S(1)}, bf16[48,24,222]{2,1,0:T(8,128)(2,1)S(1)}) fusion(bf16[48,24,222]{2,1,0:T(8,128)(2,1)} %param.7, bf16[48,24,222]{2,1,0:T(8,128)(2,1)} %param.6, bf16[48,24,222]{2,1,0:T(8,128)(2,1)} %param.5), kind=kLoop, calls=%fused_computation.6 | loop fusion | flops 1790208 | bytes 2557440 | tf_op jit(solution)/shard_map/convert_element_type | solution.py:175
  1.7 0.0 copy-start.1
  1.7 0.6 fusion.6
  2.4 0.1 copy-done.1
  2.4 0.1 copy.7
  2.5 0.1 broadcast_in_dim.26
  2.6 0.6 fusion.1
  3.2 0.0 copy-start
  3.3 29.5 %shard_map.55.got = bf16[32,16,1152]{2,1,0:T(8,128)(2,1)S(1)} custom-call(bf16[32,16,1152]{2,1,0:T(8,128)(2,1)S(1)} %bitcast.8), custom_call_target="tpu_custom_call" | custom-call | tf_op jit(solution)/shard_map/pallas_call | solution.py:61
  32.8 0.0 copy-done
  32.9 21.0 %shard_map.56.src = f32[32,8,128]{2,1,0:T(8,128)S(1)} custom-call(s32[8]{0:T(128)S(1)} %copy-done, f32[96]{0:T(128)S(1)} %multiply_cosine_fusion.weights, bf16[32,16,1152]{2,1,0:T(8,128)(2,1)S(1)} %shard_map.55.got), custom_call_target="tpu_custom_call" | custom-call | tf_op jit(solution)/shard_map/pallas_call | solution.py:199
  53.8 13.6 %shard_map.57 = f32[32,8,128]{2,1,0:T(8,128)S(1)} custom-call(f32[32,8,128]{2,1,0:T(8,128)S(1)} %shard_map.56.src), custom_call_target="tpu_custom_call" | custom-call | tf_op jit(solution)/shard_map/pallas_call | solution.py:61
  67.5 0.2 reshape.62
  67.8 0.8 %copy.8 = f32[4,24,222]{2,1,0:T(8,128)} copy(f32[4,24,222]{1,0,2:T(4,128)S(1)} %slice_bitcast_fusion) | data formatting | bytes 170496 | tf_op jit(solution)/shard_map/transpose | solution.py:220
  (6 shorter events, 0.1 us)
Async XLA Ops:
  1.7 0.7 %copy-start.1 = (s32[48,24]{0,1:T(8,128)S(1)}, s32[48,24]{0,1:T(8,128)}, u32[]{:S(2)}) copy-start(s32[48,24]{0,1:T(8,128)} %param.8) | copy-start | bytes 13828
  3.2 29.6 %copy-start = (s32[8]{0:T(128)S(1)}, s32[8]{0:T(128)}, u32[]{:S(2)}) copy-start(s32[8]{0:T(128)} %offsets.1) | copy-start | bytes 100

commit v2 on v0

--- a/solution.py
+++ b/solution.py
@@ -1,12 +1,311 @@
+import functools
+import math
+
 import jax
 import jax.numpy as jnp
 from jax import lax
+from jax.experimental import pallas as pl
+from jax.experimental.pallas import tpu as pltpu
 from jax.sharding import PartitionSpec as P
 
+MESH = pl.DeviceIdType.MESH
+LANES = 128
+SLOTS = 8
+UNUSABLE = 1024.0
+LIMIT = 512.0
+regular_term = 0.001
+
+
+def rank_of(u, n, groups):
+    return ((u + 1) * n + groups - 1) // groups - 1
+
+
+def lag_kernel(sizes, offsets, weights, sent, back, got, fore_w, fore_ww, weight, truth, truth_b, spread, move, total, found,
+               send_sem, recv_sem, own_sem, result_sem, back_sem, last_sem):
+    n_lat, n_lon, rows, cols, lags, groups = sizes
+    n = n_lat * n_lon
+    tiles = n_lon * cols // LANES
+    group = math.lcm(cols, LANES) // cols
+    phases = rows // group
+    width = group * cols
+    per_owner = lags // n_lat
+    me = lax.axis_index("lon") * n_lat + lax.axis_index("lat")
+    mine = me * groups // n
+    active = (me + 1) * groups // n > mine
+
+    def place(rank):
+        return {"lat": rank % n_lat, "lon": rank // n_lat}
+
+    def part(b):
+        return pl.ds(pl.multiple_of(b * width, LANES), width)
+
+    barrier = pltpu.get_barrier_semaphore()
+
+    def greet(o, _):
+        pl.semaphore_signal(barrier, inc=1, device_id=place((me + o) % n), device_id_type=MESH)
+        return 0
+
+    lax.fori_loop(1, n, greet, 0)
+
+    def own(b):
+        return pltpu.make_async_copy(
+            sent.at[mine, :, part(b)], got.at[me, :, part(b)], own_sem.at[b]
+        )
+
+    @pl.when(active)
+    def _():
+        for b in range(phases):
+            own(b).start()
+
+    total[...] = jnp.zeros_like(total)
+    found[...] = jnp.zeros_like(found)
+    pl.semaphore_wait(barrier, n - 1)
+
+    def outgoing(b, u):
+        return pltpu.make_async_remote_copy(
+            src_ref=sent.at[u, :, part(b)],
+            dst_ref=got.at[me, :, part(b)],
+            send_sem=send_sem.at[b, u],
+            recv_sem=recv_sem.at[b, me],
+            device_id=place(rank_of(u, n, groups)),
+            device_id_type=MESH,
+        )
+
+    def arriving(b, rank):
+        return pltpu.make_async_remote_copy(
+            src_ref=got.at[rank, :, part(b)],
+            dst_ref=got.at[rank, :, part(b)],
+            send_sem=send_sem.at[b, 0],
+            recv_sem=recv_sem.at[b, rank],
+            device_id=place(rank),
+            device_id_type=MESH,
+        )
+
+    for b in range(phases):
+
+        def start(o, _, b=b):
+            u = (mine + o) % groups
+
+            @pl.when(rank_of(u, n, groups) != me)
+            def _():
+                outgoing(b, u).start()
+
+            return 0
+
+        lax.fori_loop(0, groups, start, 0)
+
+    total_cols = n_lon * cols
+    distance = lax.broadcasted_iota(jnp.int32, (total_cols, total_cols), 0) - lax.broadcasted_iota(
+        jnp.int32, (total_cols, total_cols), 1
+    )
+    distance = jnp.where(distance < 0, distance + total_cols, distance)
+    spread[...] = distance
+
+    def build(k, _):
+        move[k] = jnp.where(spread[...] == offsets[k], 1.0, 0.0).astype(jnp.bfloat16)
+        return 0
+
+    lax.fori_loop(0, lags, build, 0)
+    zero = jnp.zeros((SLOTS, LANES), jnp.float32)
+
+    def phase(b, _):
+        def arrive(o, _):
+            arriving(b, (me + o) % n).wait_recv()
+            return 0
+
+        own(b).wait()
+        lax.fori_loop(1, n, arrive, 0)
+
+        def unpack(half, _):
+            for d in range(n_lon):
+                chunk = got[d * n_lat + half, :, part(b)].astype(jnp.float32)
+                for i in range(group):
+                    piece = chunk[:, i * cols : (i + 1) * cols]
+                    fore_w[half * group + i, :, d * cols : (d + 1) * cols] = piece[:SLOTS]
+                    truth[half * group + i, :, d * cols : (d + 1) * cols] = piece[SLOTS:]
+            return 0
+
+        lax.fori_loop(0, n_lat, unpack, 0)
+
+        def prepare(i, _):
+            w = weights[i // group * rows + b * group + i % group]
+            for m in range(tiles):
+                at = pl.ds(m * LANES, LANES)
+                fore = fore_w[i, :, at]
+                usable = fore < LIMIT
+                fore = jnp.where(usable, fore, 0.0)
+                weighted = w * fore
+                weight[i, :, at] = jnp.where(usable, w, 0.0)
+                fore_w[i, :, at] = weighted
+                fore_ww[i, :, at] = weighted * fore
+            return 0
+
+        lax.fori_loop(0, n_lat * group, prepare, 0, unroll=2)
+
+        truth_b[...] = truth[...].reshape(truth_b.shape).astype(jnp.bfloat16)
+
+        def lag(k, _):
+            shifted = jnp.dot(truth_b[...], move[k], preferred_element_type=jnp.float32)
+            for m in range(tiles):
+                at = slice(m * LANES, (m + 1) * LANES)
+                cov = var_fore = var_true = zero
+                for i in range(n_lat * group):
+                    true = shifted[i * SLOTS : (i + 1) * SLOTS, at]
+                    seen = true < LIMIT
+                    true = jnp.where(seen, true, 0.0)
+                    cov += fore_w[i, :, at] * true
+                    var_fore += jnp.where(seen, fore_ww[i, :, at], 0.0)
+                    var_true += weight[i, :, at] * (true * true)
+                total[k, 0, :, at] += cov
+                total[k, 1, :, at] += var_fore
+                total[k, 2, :, at] += var_true
+            return 0
+
+        lax.fori_loop(0, lags, lag, 0)
+        return 0
+
+    def returning(rank):
+        return pltpu.make_async_remote_copy(
+            src_ref=found.at[rank],
+            dst_ref=back.at[mine],
+            send_sem=result_sem.at[rank],
+            recv_sem=back_sem.at[mine],
+            device_id=place(rank),
+            device_id_type=MESH,
+        )
+
+    def returned(u):
+        return pltpu.make_async_remote_copy(
+            src_ref=back.at[u],
+            dst_ref=back.at[u],
+            send_sem=result_sem.at[0],
+            recv_sem=back_sem.at[u],
+            device_id=place(rank_of(u, n, groups)),
+            device_id_type=MESH,
+        )
+
+    last = pltpu.make_async_copy(found.at[me], back.at[mine], last_sem)
+
+    @pl.when(active)
+    def _():
+        lax.fori_loop(0, phases, phase, 0)
+        for k in range(lags):
+            cov, var_fore, var_true = total[k, 0], total[k, 1], total[k, 2]
+            value = cov / jnp.sqrt((var_fore + regular_term) * (var_true + regular_term))
+            owner, at = k // per_owner, k % per_owner
+            for d in range(n_lon):
+                found[d * n_lat + owner, :, at * cols : (at + 1) * cols] = value[
+                    :, d * cols : (d + 1) * cols
+                ]
+
+        def send_back(o, _):
+            returning((me + o) % n).start()
+            return 0
+
+        lax.fori_loop(1, n, send_back, 0)
+        last.start()
+
+        def sent_back(o, _):
+            returning((me + o) % n).wait_send()
+            return 0
+
+        lax.fori_loop(1, n, sent_back, 0)
+        last.wait()
+
+    def finish(u, _):
+        @pl.when(rank_of(u, n, groups) != me)
+        def _():
+            for b in range(phases):
+                outgoing(b, u).wait_send()
+            returned(u).wait_recv()
+
+        return 0
+
+    lax.fori_loop(0, groups, finish, 0)
+
+
+def by_channel(n_lat, n_lon, prediction, observed_state, mean_state, usable_point_flags, offsets):
+    rows, cols, channels = prediction.shape
+    lags = offsets.shape[0]
+    n = n_lat * n_lon
+    groups = -(-channels // SLOTS)
+    points = rows * cols
+    total_rows, total_cols = rows * n_lat, cols * n_lon
+    mean = mean_state.astype(jnp.float32)
+    fore = (prediction.astype(jnp.float32) - mean).astype(jnp.bfloat16).reshape(points, channels)
+    true = (observed_state.astype(jnp.float32) - mean).astype(jnp.bfloat16).reshape(points, channels)
+
+    index = jnp.arange(groups * 2 * SLOTS, dtype=jnp.int32)
+    owner, slot = index // (2 * SLOTS), index % (2 * SLOTS)
+    wanted = (owner * SLOTS + slot % SLOTS)[:, None]
+    hit = wanted == jnp.arange(channels, dtype=jnp.int32)[None, :]
+    pick_fore = (hit & (slot < SLOTS)[:, None]).astype(jnp.bfloat16)
+    pick_true = (hit & (slot >= SLOTS)[:, None]).astype(jnp.bfloat16)
+    turn = functools.partial(
+        lax.dot_general,
+        dimension_numbers=(((1,), (1,)), ((), ())),
+        preferred_element_type=jnp.float32,
+    )
+    packed = turn(pick_fore, fore) + turn(pick_true, true)
+    flags = usable_point_flags.reshape(1, points)
+    packed = jnp.where(flags != 0, packed, UNUSABLE).astype(jnp.bfloat16)
+    packed = packed.reshape(groups, 2 * SLOTS, points)
+
+    row_index = jnp.arange(total_rows, dtype=jnp.int32).astype(jnp.float32)
+    weights = jnp.cos(jnp.pi * ((row_index + 0.5) / total_rows - 0.5))
+    group = math.lcm(cols, LANES) // cols
+    phases = rows // group
+    held = (n_lat * group, SLOTS, total_cols)
+    back = pl.pallas_call(
+        functools.partial(lag_kernel, (n_lat, n_lon, rows, cols, lags, groups)),
+        out_shape=jax.ShapeDtypeStruct((groups, SLOTS, LANES), jnp.float32),
+        in_specs=[
+            pl.BlockSpec(memory_space=pltpu.SMEM),
+            pl.BlockSpec(memory_space=pltpu.SMEM),
+            pl.BlockSpec(memory_space=pltpu.VMEM),
+        ],
+        out_specs=pl.BlockSpec(memory_space=pltpu.VMEM),
+        scratch_shapes=[
+            pltpu.VMEM((n, 2 * SLOTS, points), jnp.bfloat16),
+            pltpu.VMEM(held, jnp.float32),
+            pltpu.VMEM(held, jnp.float32),
+            pltpu.VMEM(held, jnp.float32),
+            pltpu.VMEM(held, jnp.float32),
+            pltpu.VMEM((n_lat * group * SLOTS, total_cols), jnp.bfloat16),
+            pltpu.VMEM((total_cols, total_cols), jnp.int32),
+            pltpu.VMEM((lags, total_cols, total_cols), jnp.bfloat16),
+            pltpu.VMEM((lags, 3, SLOTS, total_cols), jnp.float32),
+            pltpu.VMEM((n, SLOTS, LANES), jnp.float32),
+            pltpu.SemaphoreType.DMA((phases, groups)),
+            pltpu.SemaphoreType.DMA((phases, n)),
+            pltpu.SemaphoreType.DMA((phases,)),
+            pltpu.SemaphoreType.DMA((n,)),
+            pltpu.SemaphoreType.DMA((groups,)),
+            pltpu.SemaphoreType.DMA,
+        ],
+        compiler_params=pltpu.CompilerParams(
+            collective_id=0, has_side_effects=True, vmem_limit_bytes=40 * 2**20
+        ),
+    )(offsets, weights, packed)
+
+    mine = lags // n_lat
+    back = back[:, :, : mine * cols].reshape(groups * SLOTS, mine, cols)[:channels]
+    return back.transpose(1, 2, 0)
+
+
+def fits(n_lat, n_lon, rows, cols, channels, lags):
+    n = n_lat * n_lon
+    group = math.lcm(cols, LANES) // cols
+    return (
+        -(-channels // SLOTS) <= n <= channels
+        and rows % group == 0
+        and (cols * n_lon) % LANES == 0
+        and lags % n_lat == 0
+        and lags // n_lat * cols <= LANES
+    )
+
+
 REACH = 14
-
-
-regular_term = 0.001
 
 
 def from_behind(value, axis, by):
@@ -14,7 +313,7 @@
     return lax.ppermute(value, axis, [(i, (i + by) % count) for i in range(count)])
 
 
-def local(prediction, observed_state, mean_state, usable_point_flags, eastward_offsets):
+def ring(prediction, observed_state, mean_state, usable_point_flags, eastward_offsets):
     meridian_extent, parallel_extent, field_total = prediction.shape
     total_rows = meridian_extent * lax.axis_size("lat")
     row_index = (
@@ -70,6 +369,7 @@
 
 
 def solution(mesh):
+    n_lat, n_lon = mesh.shape["lat"], mesh.shape["lon"]
     placed = (
         P("lat", "lon", None),
         P("lat", "lon", None),
@@ -77,6 +377,12 @@
         P("lat", "lon"),
         P(),
     )
+
+    def local(*args):
+        if fits(n_lat, n_lon, *args[0].shape, args[4].shape[0]):
+            return by_channel(n_lat, n_lon, *args)
+        return ring(*args)
+
     return jax.shard_map(
         local, mesh=mesh, in_specs=placed, out_specs=P("lat", "lon", None), check_vma=False
     )

time: 294 us -> 48.6 us (0.17)
  waiting for transfers between devices: 145 us -> 0 us
  starting transfers between devices: 66.5 us -> 0 us
  Pallas kernels: 0 us -> 44 us
  local copies, waits for them, and re-layouts: 35.4 us -> 1.46 us
  other arithmetic: 17.7 us -> 1.77 us
  loops' own time: 15.5 us -> 0 us
  between operations: 13.1 us -> 0.09 us
    ppermute x28 -> x0, waiting for transfers between devices: 106 us -> none  [from_behind(): lax.ppermute(value, axis, [(i, (i + by) % count) for i in range(count)])]
    ppermute x28 -> x0, starting transfers between devices: 66.5 us -> none  [from_behind(): lax.ppermute(value, axis, [(i, (i + by) % count) for i in range(count)])]
    pallas_call x0 -> x1, Pallas kernels: none -> 44 us  [by_channel(): pl.pallas_call(functools.partial(lag_kernel, (n_lat, n_lon, rows, cols, l...]
    reduce_scatter x3 -> x0, waiting for transfers between devices: 37.4 us -> none  [the longest x1 13.3 us: local(): lax.psum_scatter(var_true, 'lat', scatter_dimension=0, tiled=True)]
    dynamic_update_slice x46 -> x0, local copies, waits for them, and re-layouts: 28.6 us -> none  [the longest x14 12.7 us: advance(): lax.dynamic_update_slice_in_dim(buffer_true, slab_true, place, 1)]
    another operation x2 -> x0, loops' own time: 15.5 us -> none  [the longest x1 15.1 us: local(): lax.map(lag_sums, eastward_offsets)]
    reduce_sum x8 -> x0, other arithmetic: 13.7 us -> none  [lag_sums(): var_true = jnp.sum(couple_factor * frame_segment * frame_segment, axis=0)]
    dynamic_slice x8 -> x0, local copies, waits for them, and re-layouts: 4.76 us -> none  [local(): lax.map(lag_sums, eastward_offsets)]
  transfers between devices with their start and end apart: 31 -> 0, of which waited for: 17 -> 0; matrix products, arithmetic and copies ran while one was open for 2% -> 0% of each run, Pallas kernels for 0% -> 0%
where the time goes in v2:
time: 48.6 us; the launch traced here: 48.4 us
  Pallas kernels  44 us (91%)
  other arithmetic  1.77 us (4%)
  local copies, waits for them, and re-layouts  1.46 us (3%)
  matrix products  1.04 us (2%)
    pallas_call x1, Pallas kernels, by_channel(): pl.pallas_call(functools.partial(lag_kernel, (n_lat, n_lon, rows, cols, l...  44 us
    convert_element_type x1, other arithmetic, by_channel(): (observed_state.astype(jnp.float32) - mean).astype(jnp.bfloat16)  1.7 us
    dot_general x2, matrix products, by_channel(): packed = turn(pick_fore, fore) + turn(pick_true, true)  1.04 us

profile of v2, /device:TPU:0, one launch (start us, length us, event | category | flops | bytes accessed | tf_op | source)
XLA Modules:
  0.0 48.4 jit_solution(10630611347304426871)
XLA Ops:
  0.0 1.7 %fusion.3 = (bf16[48,24,222]{2,1,0:T(8,128)(2,1)S(1)}, bf16[48,24,222]{2,1,0:T(8,128)(2,1)S(1)}) fusion(bf16[48,24,222]{2,1,0:T(8,128)(2,1)} %param.7, bf16[48,24,222]{2,1,0:T(8,128)(2,1)} %param.6, bf16[48,24,222]{2,1,0:T(8,128)(2,1)} %param.5), kind=kLoop, calls=%fused_computation.6 | loop fusion | flops 1790208 | bytes 2557440 | tf_op jit(solution)/shard_map/convert_element_type | solution.py:236
  1.7 0.0 copy-start.1
  1.7 0.5 %fusion.6 = f32[448,1152]{1,0:T(8,128)S(1)} fusion(bf16[1152,222]{1,0:T(8,128)(2,1)S(1)} %bitcast.10, s32[448]{0:T(512)S(1)} %fusion.18, pred[448]{0:T(512)(128)(4,1)S(1)} %broadcast_compare_fusion.1), kind=kOutput, calls=%fused_computation.10 | convolution fusion | flops 229345536 | bytes 2578112 | tf_op jit(solution)/shard_map/dot_general | solution.py:249
  2.2 0.0 copy-start
  2.3 0.1 copy-done.1
  2.4 0.1 copy.7
  2.5 0.1 ne.85
  2.6 0.5 %fusion.1 = bf16[448,1152]{1,0:T(8,128)(2,1)S(1)} fusion(f32[448,1152]{1,0:T(8,128)S(1)} %fusion.6, bf16[1152,222]{1,0:T(8,128)(2,1)S(1)} %bitcast.11, pred[1152]{0:T(1024)(128)(4,1)S(1)} %ne.85, s32[448]{0:T(512)S(1)} %fusion.18, pred[448]{0:T(512)(128)(4,1)S(1)} %broadcast_compare_fusion.2), kind=kOutput, calls=%fused_computation.2 | convolution fusion | flops 230893824 | bytes 3611456 | tf_op jit(solution)/shard_map/dot_general | solution.py:249
  3.2 0.0 copy-done
  3.2 44.0 %shard_map.55 = f32[28,8,128]{2,1,0:T(8,128)S(1)} custom-call(s32[8]{0:T(128)S(1)} %copy-done, f32[96]{0:T(128)S(1)} %multiply_cosine_fusion.weights, bf16[28,16,1152]{2,1,0:T(8,128)(2,1)S(1)} %bitcast.8), custom_call_target="tpu_custom_call" | custom-call | tf_op jit(solution)/shard_map/pallas_call | solution.py:259
  47.3 0.2 reshape.64
  47.5 0.8 %copy.8 = f32[4,24,222]{2,1,0:T(8,128)} copy(f32[4,24,222]{1,0,2:T(4,128)S(1)} %slice_bitcast_fusion) | data formatting | bytes 170496 | tf_op jit(solution)/shard_map/transpose | solution.py:293
  (6 shorter events, 0.1 us)
Async XLA Ops:
  1.7 0.7 %copy-start.1 = (s32[48,24]{0,1:T(8,128)S(1)}, s32[48,24]{0,1:T(8,128)}, u32[]{:S(2)}) copy-start(s32[48,24]{0,1:T(8,128)} %param.8) | copy-start | bytes 13828
  2.2 1.0 %copy-start = (s32[8]{0:T(128)S(1)}, s32[8]{0:T(128)}, u32[]{:S(2)}) copy-start(s32[8]{0:T(128)} %offsets.1) | copy-start | bytes 100

commit v3 on v2

--- a/solution.py
+++ b/solution.py
@@ -20,7 +20,7 @@
     return ((u + 1) * n + groups - 1) // groups - 1
 
 
-def lag_kernel(sizes, offsets, weights, sent, back, got, fore_w, fore_ww, weight, truth, truth_b, spread, move, total, found,
+def lag_kernel(sizes, offsets, weights, sent, back, got, fore_w, fore_ww, weight, truth, total, found,
                send_sem, recv_sem, own_sem, result_sem, back_sem, last_sem):
     n_lat, n_lon, rows, cols, lags, groups = sizes
     n = n_lat * n_lon
@@ -84,7 +84,7 @@
     for b in range(phases):
 
         def start(o, _, b=b):
-            u = (mine + o) % groups
+            u = (mine + o // 2 + o % 2 * ((groups + 1) // 2)) % groups
 
             @pl.when(rank_of(u, n, groups) != me)
             def _():
@@ -94,18 +94,7 @@
 
         lax.fori_loop(0, groups, start, 0)
 
-    total_cols = n_lon * cols
-    distance = lax.broadcasted_iota(jnp.int32, (total_cols, total_cols), 0) - lax.broadcasted_iota(
-        jnp.int32, (total_cols, total_cols), 1
-    )
-    distance = jnp.where(distance < 0, distance + total_cols, distance)
-    spread[...] = distance
-
-    def build(k, _):
-        move[k] = jnp.where(spread[...] == offsets[k], 1.0, 0.0).astype(jnp.bfloat16)
-        return 0
-
-    lax.fori_loop(0, lags, build, 0)
+    lane = lax.broadcasted_iota(jnp.int32, (SLOTS, LANES), 1)
     zero = jnp.zeros((SLOTS, LANES), jnp.float32)
 
     def phase(b, _):
@@ -142,23 +131,37 @@
 
         lax.fori_loop(0, n_lat * group, prepare, 0, unroll=2)
 
-        truth_b[...] = truth[...].reshape(truth_b.shape).astype(jnp.bfloat16)
-
         def lag(k, _):
-            shifted = jnp.dot(truth_b[...], move[k], preferred_element_type=jnp.float32)
+            shift = offsets[k]
+            first, turn = lax.div(shift, LANES), lax.rem(shift, LANES)
+            stay = lane < LANES - turn
+            sums = [(zero, zero, zero)] * tiles
+            for i in range(n_lat * group):
+                turned = [
+                    pltpu.roll(truth[i, :, m * LANES : (m + 1) * LANES], LANES - turn, 1)
+                    for m in range(tiles)
+                ]
+                ahead = []
+                for m in range(tiles):
+                    value = turned[m]
+                    for f in range(1, tiles):
+                        value = jnp.where(first == f, turned[(m + f) % tiles], value)
+                    ahead.append(value)
+                for m in range(tiles):
+                    at = slice(m * LANES, (m + 1) * LANES)
+                    true = jnp.where(stay, ahead[m], ahead[(m + 1) % tiles])
+                    seen = true < LIMIT
+                    true = jnp.where(seen, true, 0.0)
+                    cov, var_fore, var_true = sums[m]
+                    sums[m] = (
+                        cov + fore_w[i, :, at] * true,
+                        var_fore + jnp.where(seen, fore_ww[i, :, at], 0.0),
+                        var_true + weight[i, :, at] * (true * true),
+                    )
             for m in range(tiles):
                 at = slice(m * LANES, (m + 1) * LANES)
-                cov = var_fore = var_true = zero
-                for i in range(n_lat * group):
-                    true = shifted[i * SLOTS : (i + 1) * SLOTS, at]
-                    seen = true < LIMIT
-                    true = jnp.where(seen, true, 0.0)
-                    cov += fore_w[i, :, at] * true
-                    var_fore += jnp.where(seen, fore_ww[i, :, at], 0.0)
-                    var_true += weight[i, :, at] * (true * true)
-                total[k, 0, :, at] += cov
-                total[k, 1, :, at] += var_fore
-                total[k, 2, :, at] += var_true
+                for q in range(3):
+                    total[k, q, :, at] += sums[m][q]
             return 0
 
         lax.fori_loop(0, lags, lag, 0)
@@ -271,9 +274,6 @@
             pltpu.VMEM(held, jnp.float32),
             pltpu.VMEM(held, jnp.float32),
             pltpu.VMEM(held, jnp.float32),
-            pltpu.VMEM((n_lat * group * SLOTS, total_cols), jnp.bfloat16),
-            pltpu.VMEM((total_cols, total_cols), jnp.int32),
-            pltpu.VMEM((lags, total_cols, total_cols), jnp.bfloat16),
             pltpu.VMEM((lags, 3, SLOTS, total_cols), jnp.float32),
             pltpu.VMEM((n, SLOTS, LANES), jnp.float32),
             pltpu.SemaphoreType.DMA((phases, groups)),

time: 48.6 us -> 46.9 us (0.965)
  Pallas kernels: 44 us -> 42.3 us
    pallas_call x1, Pallas kernels: 44 us -> 42.3 us  [by_channel(): pl.pallas_call(functools.partial(lag_kernel, (n_lat, n_lon, rows, cols, l...]
where the time goes in v3:
time: 46.9 us; the launch traced here: 46.7 us
  Pallas kernels  42.3 us (90%)
  other arithmetic  1.77 us (4%)
  local copies, waits for them, and re-layouts  1.46 us (3%)
  matrix products  1.04 us (2%)
    pallas_call x1, Pallas kernels, by_channel(): pl.pallas_call(functools.partial(lag_kernel, (n_lat, n_lon, rows, cols, l...  42.3 us
    convert_element_type x1, other arithmetic, by_channel(): (observed_state.astype(jnp.float32) - mean).astype(jnp.bfloat16)  1.7 us
    dot_general x2, matrix products, by_channel(): packed = turn(pick_fore, fore) + turn(pick_true, true)  1.04 us

profile of v3, /device:TPU:0, one launch (start us, length us, event | category | flops | bytes accessed | tf_op | source)
XLA Modules:
  0.0 46.7 jit_solution(15066556871672368124)
XLA Ops:
  0.0 1.7 %fusion.3 = (bf16[48,24,222]{2,1,0:T(8,128)(2,1)S(1)}, bf16[48,24,222]{2,1,0:T(8,128)(2,1)S(1)}) fusion(bf16[48,24,222]{2,1,0:T(8,128)(2,1)} %param.7, bf16[48,24,222]{2,1,0:T(8,128)(2,1)} %param.6, bf16[48,24,222]{2,1,0:T(8,128)(2,1)} %param.5), kind=kLoop, calls=%fused_computation.6 | loop fusion | flops 1790208 | bytes 2557440 | tf_op jit(solution)/shard_map/convert_element_type | solution.py:239
  1.7 0.0 copy-start.1
  1.7 0.5 %fusion.6 = f32[448,1152]{1,0:T(8,128)S(1)} fusion(bf16[1152,222]{1,0:T(8,128)(2,1)S(1)} %bitcast.10, s32[448]{0:T(512)S(1)} %fusion.18, pred[448]{0:T(512)(128)(4,1)S(1)} %broadcast_compare_fusion.1), kind=kOutput, calls=%fused_computation.10 | convolution fusion | flops 229345536 | bytes 2578112 | tf_op jit(solution)/shard_map/dot_general | solution.py:252
  2.2 0.0 copy-start
  2.3 0.1 copy-done.1
  2.4 0.1 copy.7
  2.5 0.1 ne.85
  2.6 0.5 %fusion.1 = bf16[448,1152]{1,0:T(8,128)(2,1)S(1)} fusion(f32[448,1152]{1,0:T(8,128)S(1)} %fusion.6, bf16[1152,222]{1,0:T(8,128)(2,1)S(1)} %bitcast.11, pred[1152]{0:T(1024)(128)(4,1)S(1)} %ne.85, s32[448]{0:T(512)S(1)} %fusion.18, pred[448]{0:T(512)(128)(4,1)S(1)} %broadcast_compare_fusion.2), kind=kOutput, calls=%fused_computation.2 | convolution fusion | flops 230893824 | bytes 3611456 | tf_op jit(solution)/shard_map/dot_general | solution.py:252
  3.2 0.0 copy-done
  3.2 42.3 %shard_map.55 = f32[28,8,128]{2,1,0:T(8,128)S(1)} custom-call(s32[8]{0:T(128)S(1)} %copy-done, f32[96]{0:T(128)S(1)} %multiply_cosine_fusion.weights, bf16[28,16,1152]{2,1,0:T(8,128)(2,1)S(1)} %bitcast.8), custom_call_target="tpu_custom_call" | custom-call | tf_op jit(solution)/shard_map/pallas_call | solution.py:262
  45.6 0.2 reshape.64
  45.8 0.8 %copy.8 = f32[4,24,222]{2,1,0:T(8,128)} copy(f32[4,24,222]{1,0,2:T(4,128)S(1)} %slice_bitcast_fusion) | data formatting | bytes 170496 | tf_op jit(solution)/shard_map/transpose | solution.py:293
  (6 shorter events, 0.1 us)
Async XLA Ops:
  1.7 0.7 %copy-start.1 = (s32[48,24]{0,1:T(8,128)S(1)}, s32[48,24]{0,1:T(8,128)}, u32[]{:S(2)}) copy-start(s32[48,24]{0,1:T(8,128)} %param.8) | copy-start | bytes 13828
  2.2 1.0 %copy-start = (s32[8]{0:T(128)S(1)}, s32[8]{0:T(128)}, u32[]{:S(2)}) copy-start(s32[8]{0:T(128)} %offsets.1) | copy-start | bytes 100

commit v4 on v3

--- a/solution.py
+++ b/solution.py
@@ -20,8 +20,9 @@
     return ((u + 1) * n + groups - 1) // groups - 1
 
 
-def lag_kernel(sizes, offsets, weights, sent, back, got, fore_w, fore_ww, weight, truth, total, found,
-               send_sem, recv_sem, own_sem, result_sem, back_sem, last_sem):
+def lag_kernel(sizes, offsets, weights, flags, prediction, observed, mean, out,
+               fields, sent, back, got, fore_w, fore_ww, weight, truth, total, found,
+               load_sem, send_sem, recv_sem, own_sem, result_sem, back_sem, last_sem):
     n_lat, n_lon, rows, cols, lags, groups = sizes
     n = n_lat * n_lon
     tiles = n_lon * cols // LANES
@@ -47,16 +48,53 @@
 
     lax.fori_loop(1, n, greet, 0)
 
+    def load(b):
+        at = pl.ds(b * group, group)
+        return [
+            pltpu.make_async_copy(source.at[at], fields.at[q, at], load_sem.at[q, b])
+            for q, source in enumerate((prediction, observed, mean))
+        ]
+
+    for b in range(phases):
+        for copy in load(b):
+            copy.start()
+
+    channels = prediction.shape[2]
+    identity = jnp.where(
+        lax.broadcasted_iota(jnp.int32, (groups * SLOTS, channels), 0)
+        == lax.broadcasted_iota(jnp.int32, (groups * SLOTS, channels), 1),
+        1.0,
+        0.0,
+    ).astype(jnp.bfloat16)
+
+    def pack(b):
+        for copy in load(b):
+            copy.wait()
+        fore, true = [], []
+        for i in range(b * group, (b + 1) * group):
+            usable = jnp.broadcast_to(flags[:, i : i + 1], (cols, channels)) != 0
+            middle = fields[2, i].astype(jnp.float32)
+            fore.append(jnp.where(usable, fields[0, i].astype(jnp.float32) - middle, UNUSABLE))
+            true.append(jnp.where(usable, fields[1, i].astype(jnp.float32) - middle, UNUSABLE))
+        turned = [
+            lax.dot_general(
+                identity,
+                jnp.concatenate(values, axis=0).astype(jnp.bfloat16),
+                (((1,), (1,)), ((), ())),
+                preferred_element_type=jnp.float32,
+            ).reshape(groups, SLOTS, width)
+            for values in (fore, true)
+        ]
+        sent[:, :, b * width : (b + 1) * width] = jnp.concatenate(turned, axis=1).astype(
+            jnp.bfloat16
+        )
+
     def own(b):
         return pltpu.make_async_copy(
             sent.at[mine, :, part(b)], got.at[me, :, part(b)], own_sem.at[b]
         )
 
-    @pl.when(active)
-    def _():
-        for b in range(phases):
-            own(b).start()
-
+    pack(0)
     total[...] = jnp.zeros_like(total)
     found[...] = jnp.zeros_like(found)
     pl.semaphore_wait(barrier, n - 1)
@@ -82,6 +120,12 @@
         )
 
     for b in range(phases):
+        if b > 0:
+            pack(b)
+
+        @pl.when(active)
+        def _(b=b):
+            own(b).start()
 
         def start(o, _, b=b):
             u = (mine + o // 2 + o % 2 * ((groups + 1) // 2)) % groups
@@ -135,10 +179,11 @@
             shift = offsets[k]
             first, turn = lax.div(shift, LANES), lax.rem(shift, LANES)
             stay = lane < LANES - turn
+            back_turn = lax.rem(LANES - turn, LANES)
             sums = [(zero, zero, zero)] * tiles
             for i in range(n_lat * group):
                 turned = [
-                    pltpu.roll(truth[i, :, m * LANES : (m + 1) * LANES], LANES - turn, 1)
+                    pltpu.roll(truth[i, :, m * LANES : (m + 1) * LANES], back_turn, 1)
                     for m in range(tiles)
                 ]
                 ahead = []
@@ -213,7 +258,6 @@
             return 0
 
         lax.fori_loop(1, n, sent_back, 0)
-        last.wait()
 
     def finish(u, _):
         @pl.when(rank_of(u, n, groups) != me)
@@ -225,6 +269,13 @@
         return 0
 
     lax.fori_loop(0, groups, finish, 0)
+
+    @pl.when(active)
+    def _():
+        last.wait()
+
+    correlation = back[...].reshape(groups * SLOTS, LANES).T
+    out[...] = correlation[: per_owner * cols, :channels]
 
 
 def by_channel(n_lat, n_lon, prediction, observed_state, mean_state, usable_point_flags, offsets):
@@ -234,41 +285,28 @@
     groups = -(-channels // SLOTS)
     points = rows * cols
     total_rows, total_cols = rows * n_lat, cols * n_lon
-    mean = mean_state.astype(jnp.float32)
-    fore = (prediction.astype(jnp.float32) - mean).astype(jnp.bfloat16).reshape(points, channels)
-    true = (observed_state.astype(jnp.float32) - mean).astype(jnp.bfloat16).reshape(points, channels)
-
-    index = jnp.arange(groups * 2 * SLOTS, dtype=jnp.int32)
-    owner, slot = index // (2 * SLOTS), index % (2 * SLOTS)
-    wanted = (owner * SLOTS + slot % SLOTS)[:, None]
-    hit = wanted == jnp.arange(channels, dtype=jnp.int32)[None, :]
-    pick_fore = (hit & (slot < SLOTS)[:, None]).astype(jnp.bfloat16)
-    pick_true = (hit & (slot >= SLOTS)[:, None]).astype(jnp.bfloat16)
-    turn = functools.partial(
-        lax.dot_general,
-        dimension_numbers=(((1,), (1,)), ((), ())),
-        preferred_element_type=jnp.float32,
-    )
-    packed = turn(pick_fore, fore) + turn(pick_true, true)
-    flags = usable_point_flags.reshape(1, points)
-    packed = jnp.where(flags != 0, packed, UNUSABLE).astype(jnp.bfloat16)
-    packed = packed.reshape(groups, 2 * SLOTS, points)
-
     row_index = jnp.arange(total_rows, dtype=jnp.int32).astype(jnp.float32)
     weights = jnp.cos(jnp.pi * ((row_index + 0.5) / total_rows - 0.5))
     group = math.lcm(cols, LANES) // cols
     phases = rows // group
     held = (n_lat * group, SLOTS, total_cols)
-    back = pl.pallas_call(
+    mine = lags // n_lat
+    found = pl.pallas_call(
         functools.partial(lag_kernel, (n_lat, n_lon, rows, cols, lags, groups)),
-        out_shape=jax.ShapeDtypeStruct((groups, SLOTS, LANES), jnp.float32),
+        out_shape=jax.ShapeDtypeStruct((mine * cols, channels), jnp.float32),
         in_specs=[
             pl.BlockSpec(memory_space=pltpu.SMEM),
             pl.BlockSpec(memory_space=pltpu.SMEM),
             pl.BlockSpec(memory_space=pltpu.VMEM),
+            pl.BlockSpec(memory_space=pl.ANY),
+            pl.BlockSpec(memory_space=pl.ANY),
+            pl.BlockSpec(memory_space=pl.ANY),
         ],
         out_specs=pl.BlockSpec(memory_space=pltpu.VMEM),
         scratch_shapes=[
+            pltpu.VMEM((3, rows, cols, channels), jnp.bfloat16),
+            pltpu.VMEM((groups, 2 * SLOTS, points), jnp.bfloat16),
+            pltpu.VMEM((groups, SLOTS, LANES), jnp.float32),
             pltpu.VMEM((n, 2 * SLOTS, points), jnp.bfloat16),
             pltpu.VMEM(held, jnp.float32),
             pltpu.VMEM(held, jnp.float32),
@@ -276,6 +314,7 @@
             pltpu.VMEM(held, jnp.float32),
             pltpu.VMEM((lags, 3, SLOTS, total_cols), jnp.float32),
             pltpu.VMEM((n, SLOTS, LANES), jnp.float32),
+            pltpu.SemaphoreType.DMA((3, phases)),
             pltpu.SemaphoreType.DMA((phases, groups)),
             pltpu.SemaphoreType.DMA((phases, n)),
             pltpu.SemaphoreType.DMA((phases,)),
@@ -284,13 +323,10 @@
             pltpu.SemaphoreType.DMA,
         ],
         compiler_params=pltpu.CompilerParams(
-            collective_id=0, has_side_effects=True, vmem_limit_bytes=40 * 2**20
+            collective_id=0, has_side_effects=True, vmem_limit_bytes=60 * 2**20
         ),
-    )(offsets, weights, packed)
-
-    mine = lags // n_lat
-    back = back[:, :, : mine * cols].reshape(groups * SLOTS, mine, cols)[:channels]
-    return back.transpose(1, 2, 0)
+    )(offsets, weights, usable_point_flags.T, prediction, observed_state, mean_state)
+    return found.reshape(mine, cols, channels)
 
 
 def fits(n_lat, n_lon, rows, cols, channels, lags):
@@ -298,6 +334,7 @@
     group = math.lcm(cols, LANES) // cols
     return (
         -(-channels // SLOTS) <= n <= channels
+        and cols % SLOTS == 0
         and rows % group == 0
         and (cols * n_lon) % LANES == 0
         and lags % n_lat == 0

time: 46.9 us -> 45.6 us (0.972)
  other arithmetic: 1.77 us -> 0.56 us
  matrix products: 1.04 us -> 0 us
  Pallas kernels: 42.3 us -> 43.3 us
    convert_element_type x1 -> x0, other arithmetic: 1.7 us -> none  [by_channel(): (observed_state.astype(jnp.float32) - mean).astype(jnp.bfloat16)]
    unnamed x4 -> x1, local copies, waits for them, and re-layouts: 0.16 us -> 1.54 us
    dot_general x2 -> x0, matrix products: 1.04 us -> none  [by_channel(): packed = turn(pick_fore, fore) + turn(pick_true, true)]
    pallas_call x1, Pallas kernels: 42.3 us -> 43.3 us  [by_channel(): pl.pallas_call(functools.partial(lag_kernel, (n_lat, n_lon, rows, cols, l...]
    transpose x2 -> x0, local copies, waits for them, and re-layouts: 0.87 us -> none  [by_channel(): return back.transpose(1, 2, 0)]
    cos x1, other arithmetic: 0.05 us -> 0.56 us  [by_channel(): weights = jnp.cos(jnp.pi * ((row_index + 0.5) / total_rows - 0.5))]
where the time goes in v4:
time: 45.6 us; the launch traced here: 45.4 us
  Pallas kernels  43.3 us (95%)
  local copies, waits for them, and re-layouts  1.54 us (3%)
  other arithmetic  0.56 us (1%)
    pallas_call x1, Pallas kernels, by_channel(): pl.pallas_call(functools.partial(lag_kernel, (n_lat, n_lon, rows, cols, l...  43.3 us
    unnamed x1, local copies, waits for them, and re-layouts  1.54 us

profile of v4, /device:TPU:0, one launch (start us, length us, event | category | flops | bytes accessed | tf_op | source)
XLA Modules:
  0.0 45.4 jit_solution(3473401409453261025)
XLA Ops:
  0.0 0.6 %multiply_cosine_fusion.weights = f32[96]{0:T(128)} fusion(), kind=kLoop, calls=%fused_computation | loop fusion | flops 480 | bytes 384 | tf_op jit(solution)/shard_map/cos | solution.py:289
  0.6 43.3 %shard_map.55 = f32[96,222]{1,0:T(8,128)} custom-call(s32[8]{0:T(128)} %offsets.1, f32[96]{0:T(128)} %multiply_cosine_fusion.weights, s32[24,48]{1,0:T(8,128)} %bitcast.3, bf16[48,24,222]{2,1,0:T(8,128)(2,1)} %prediction.1, bf16[48,24,222]{2,1,0:T(8,128)(2,1)} %observed.1, bf16[48,24,222]{2,1,0:T(8,128)(2,1)} %mean.1), custom_call_target="tpu_custom_call" | custom-call | tf_op jit(solution)/shard_map/pallas_call | solution.py:294
  43.8 1.5 %copy.7 = f32[4,24,222]{2,1,0:T(8,128)} copy(f32[4,24,222]{2,1,0:T(8,128)} %bitcast.2) | data formatting | bytes 170496

commit v5 on v4

--- a/solution.py
+++ b/solution.py
@@ -21,7 +21,7 @@
 
 
 def lag_kernel(sizes, offsets, weights, flags, prediction, observed, mean, out,
-               fields, sent, back, got, fore_w, fore_ww, weight, truth, total, found,
+               fields, sent, back, got, both, fore_w, fore_ww, weight, truth, total, found,
                load_sem, send_sem, recv_sem, own_sem, result_sem, back_sem, last_sem):
     n_lat, n_lon, rows, cols, lags, groups = sizes
     n = n_lat * n_lon
@@ -142,20 +142,21 @@
     zero = jnp.zeros((SLOTS, LANES), jnp.float32)
 
     def phase(b, _):
-        def arrive(o, _):
-            arriving(b, (me + o) % n).wait_recv()
-            return 0
-
         own(b).wait()
-        lax.fori_loop(1, n, arrive, 0)
 
         def unpack(half, _):
             for d in range(n_lon):
-                chunk = got[d * n_lat + half, :, part(b)].astype(jnp.float32)
+                rank = d * n_lat + half
+
+                @pl.when(rank != me)
+                def _(rank=rank):
+                    arriving(b, rank).wait_recv()
+
+                chunk = got[rank, :, part(b)]
                 for i in range(group):
-                    piece = chunk[:, i * cols : (i + 1) * cols]
-                    fore_w[half * group + i, :, d * cols : (d + 1) * cols] = piece[:SLOTS]
-                    truth[half * group + i, :, d * cols : (d + 1) * cols] = piece[SLOTS:]
+                    both[half * group + i, :, d * cols : (d + 1) * cols] = chunk[
+                        :, i * cols : (i + 1) * cols
+                    ]
             return 0
 
         lax.fori_loop(0, n_lat, unpack, 0)
@@ -164,13 +165,15 @@
             w = weights[i // group * rows + b * group + i % group]
             for m in range(tiles):
                 at = pl.ds(m * LANES, LANES)
-                fore = fore_w[i, :, at]
+                values = both[i, :, at].astype(jnp.float32)
+                fore = values[:SLOTS]
                 usable = fore < LIMIT
                 fore = jnp.where(usable, fore, 0.0)
                 weighted = w * fore
                 weight[i, :, at] = jnp.where(usable, w, 0.0)
                 fore_w[i, :, at] = weighted
                 fore_ww[i, :, at] = weighted * fore
+                truth[i, :, at] = values[SLOTS:]
             return 0
 
         lax.fori_loop(0, n_lat * group, prepare, 0, unroll=2)
@@ -298,9 +301,9 @@
             pl.BlockSpec(memory_space=pltpu.SMEM),
             pl.BlockSpec(memory_space=pltpu.SMEM),
             pl.BlockSpec(memory_space=pltpu.VMEM),
-            pl.BlockSpec(memory_space=pl.ANY),
-            pl.BlockSpec(memory_space=pl.ANY),
-            pl.BlockSpec(memory_space=pl.ANY),
+            pl.BlockSpec(memory_space=pltpu.HBM),
+            pl.BlockSpec(memory_space=pltpu.HBM),
+            pl.BlockSpec(memory_space=pltpu.HBM),
         ],
         out_specs=pl.BlockSpec(memory_space=pltpu.VMEM),
         scratch_shapes=[
@@ -308,6 +311,7 @@
             pltpu.VMEM((groups, 2 * SLOTS, points), jnp.bfloat16),
             pltpu.VMEM((groups, SLOTS, LANES), jnp.float32),
             pltpu.VMEM((n, 2 * SLOTS, points), jnp.bfloat16),
+            pltpu.VMEM((n_lat * group, 2 * SLOTS, total_cols), jnp.bfloat16),
             pltpu.VMEM(held, jnp.float32),
             pltpu.VMEM(held, jnp.float32),
             pltpu.VMEM(held, jnp.float32),
@@ -323,7 +327,7 @@
             pltpu.SemaphoreType.DMA,
         ],
         compiler_params=pltpu.CompilerParams(
-            collective_id=0, has_side_effects=True, vmem_limit_bytes=60 * 2**20
+            collective_id=0, has_side_effects=True, vmem_limit_bytes=40 * 2**20
         ),
     )(offsets, weights, usable_point_flags.T, prediction, observed_state, mean_state)
     return found.reshape(mine, cols, channels)

time: 45.6 us -> 54.3 us (1.19)
  Pallas kernels: 43.3 us -> 48.8 us
  local copies, waits for them, and re-layouts: 1.54 us -> 5.15 us
    pallas_call x1, Pallas kernels: 43.3 us -> 48.8 us  [by_channel(): pl.pallas_call(functools.partial(lag_kernel, (n_lat, n_lon, rows, cols, l...]
    unnamed x1 -> x11, local copies, waits for them, and re-layouts: 1.54 us -> 5.15 us
where the time goes in v5:
time: 54.3 us; the launch traced here: 54 us
  Pallas kernels  48.8 us (90%)
  local copies, waits for them, and re-layouts  5.15 us (9%)
    pallas_call x1, Pallas kernels, by_channel(): pl.pallas_call(functools.partial(lag_kernel, (n_lat, n_lon, rows, cols, l...  48.8 us
    unnamed x11, local copies, waits for them, and re-layouts  5.15 us

profile of v5, /device:TPU:0, one launch (start us, length us, event | category | flops | bytes accessed | tf_op | source)
XLA Modules:
  0.0 54.0 jit_solution(17438961113344295043)
XLA Ops:
  0.0 0.0 copy-start.4
  0.0 0.6 %copy-done.4 = s32[8]{0:T(128)S(1)} copy-done((s32[8]{0:T(128)S(1)}, s32[8]{0:T(128)}, u32[]{:S(2)}) %copy-start.4) | copy-done | bytes 56
  0.7 0.0 copy-start
  0.7 1.1 %copy-done = bf16[48,24,222]{2,1,0:T(8,128)(2,1)S(1)} copy-done((bf16[48,24,222]{2,1,0:T(8,128)(2,1)S(1)}, bf16[48,24,222]{2,1,0:T(8,128)(2,1)}, u32[]{:S(2)}) %copy-start) | copy-done | bytes 511512
  1.7 0.0 copy-start.1
  1.7 1.1 %copy-done.1 = bf16[48,24,222]{2,1,0:T(8,128)(2,1)S(1)} copy-done((bf16[48,24,222]{2,1,0:T(8,128)(2,1)S(1)}, bf16[48,24,222]{2,1,0:T(8,128)(2,1)}, u32[]{:S(2)}) %copy-start.1) | copy-done | bytes 511512
  2.8 0.0 copy-start.2
  2.8 1.1 %copy-done.2 = bf16[48,24,222]{2,1,0:T(8,128)(2,1)S(1)} copy-done((bf16[48,24,222]{2,1,0:T(8,128)(2,1)S(1)}, bf16[48,24,222]{2,1,0:T(8,128)(2,1)}, u32[]{:S(2)}) %copy-start.2) | copy-done | bytes 511512
  3.9 0.0 copy-start.3
  3.9 0.7 %copy-done.3 = s32[48,24]{0,1:T(8,128)S(1)} copy-done((s32[48,24]{0,1:T(8,128)S(1)}, s32[48,24]{0,1:T(8,128)}, u32[]{:S(2)}) %copy-start.3) | copy-done | bytes 4632
  4.6 48.8 %shard_map.55 = f32[96,222]{1,0:T(8,128)S(1)} custom-call(s32[8]{0:T(128)S(1)} %copy-done.4, f32[96]{0:T(128)S(1)} %multiply_cosine_fusion.weights, s32[24,48]{1,0:T(8,128)S(1)} %bitcast.3, bf16[48,24,222]{2,1,0:T(8,128)(2,1)S(1)} %copy-done, bf16[48,24,222]{2,1,0:T(8,128)(2,1)S(1)} %copy-done.1, bf16[48,24,222]{2,1,0:T(8,128)(2,1)S(1)} %copy-done.2), custom_call_target="tpu_custom_call" | custom-call | tf_op jit(solution)/shard_map/pallas_call | solution.py:297
  53.4 0.6 %copy.7 = f32[4,24,222]{2,1,0:T(8,128)} copy(f32[4,24,222]{2,1,0:T(8,128)S(1)} %bitcast.2) | data formatting | bytes 170496
  (1 shorter events, 0.0 us)
Async XLA Ops:
  0.0 0.7 %copy-start.4 = (s32[8]{0:T(128)S(1)}, s32[8]{0:T(128)}, u32[]{:S(2)}) copy-start(s32[8]{0:T(128)} %offsets.1) | copy-start | bytes 100
  0.7 1.1 %copy-start = (bf16[48,24,222]{2,1,0:T(8,128)(2,1)S(1)}, bf16[48,24,222]{2,1,0:T(8,128)(2,1)}, u32[]{:S(2)}) copy-start(bf16[48,24,222]{2,1,0:T(8,128)(2,1)} %prediction.1) | copy-start | bytes 1534468
  1.7 1.1 %copy-start.1 = (bf16[48,24,222]{2,1,0:T(8,128)(2,1)S(1)}, bf16[48,24,222]{2,1,0:T(8,128)(2,1)}, u32[]{:S(2)}) copy-start(bf16[48,24,222]{2,1,0:T(8,128)(2,1)} %observed.1) | copy-start | bytes 1534468
  2.8 1.1 %copy-start.2 = (bf16[48,24,222]{2,1,0:T(8,128)(2,1)S(1)}, bf16[48,24,222]{2,1,0:T(8,128)(2,1)}, u32[]{:S(2)}) copy-start(bf16[48,24,222]{2,1,0:T(8,128)(2,1)} %mean.1) | copy-start | bytes 1534468
  3.9 0.7 %copy-start.3 = (s32[48,24]{0,1:T(8,128)S(1)}, s32[48,24]{0,1:T(8,128)}, u32[]{:S(2)}) copy-start(s32[48,24]{0,1:T(8,128)} %param.8) | copy-start | bytes 13828

commit v6 on v4

--- a/solution.py
+++ b/solution.py
@@ -18,6 +18,16 @@
 
 def rank_of(u, n, groups):
     return ((u + 1) * n + groups - 1) // groups - 1
+
+
+def ring_roll(tiles, by, lane):
+    count = len(tiles)
+    whole, part = by % (count * LANES) // LANES, by % LANES
+    tiles = [tiles[(m - whole) % count] for m in range(count)]
+    if part == 0:
+        return tiles
+    turned = [pltpu.roll(x, part, 1) for x in tiles]
+    return [jnp.where(lane >= part, turned[m], turned[m - 1]) for m in range(count)]
 
 
 def lag_kernel(sizes, offsets, weights, flags, prediction, observed, mean, out,
@@ -150,12 +160,34 @@
         lax.fori_loop(1, n, arrive, 0)
 
         def unpack(half, _):
-            for d in range(n_lon):
-                chunk = got[d * n_lat + half, :, part(b)].astype(jnp.float32)
+            chunks = [
+                [
+                    got[
+                        d * n_lat + half,
+                        :,
+                        pl.ds(pl.multiple_of(b * width + m * LANES, LANES), LANES),
+                    ].astype(jnp.float32)
+                    for m in range(tiles)
+                ]
+                for d in range(n_lon)
+            ]
+            for half_rows, target in ((slice(0, SLOTS), fore_w), (slice(SLOTS, None), truth)):
+                skewed = [
+                    ring_roll([x[half_rows] for x in chunks[d]], d * cols, lane)
+                    for d in range(n_lon)
+                ]
                 for i in range(group):
-                    piece = chunk[:, i * cols : (i + 1) * cols]
-                    fore_w[half * group + i, :, d * cols : (d + 1) * cols] = piece[:SLOTS]
-                    truth[half * group + i, :, d * cols : (d + 1) * cols] = piece[SLOTS:]
+                    picked = []
+                    for m in range(tiles):
+                        place_of = range(m * LANES // cols, -(-(m + 1) * LANES // cols))
+                        value = skewed[(place_of[0] - i) % group][m]
+                        for p in place_of[1:]:
+                            value = jnp.where(
+                                lane >= p * cols - m * LANES, skewed[(p - i) % group][m], value
+                            )
+                        picked.append(value)
+                    for m, value in enumerate(ring_roll(picked, -i * cols, lane)):
+                        target[half * group + i, :, m * LANES : (m + 1) * LANES] = value
             return 0
 
         lax.fori_loop(0, n_lat, unpack, 0)
@@ -298,9 +330,9 @@
             pl.BlockSpec(memory_space=pltpu.SMEM),
             pl.BlockSpec(memory_space=pltpu.SMEM),
             pl.BlockSpec(memory_space=pltpu.VMEM),
-            pl.BlockSpec(memory_space=pl.ANY),
-            pl.BlockSpec(memory_space=pl.ANY),
-            pl.BlockSpec(memory_space=pl.ANY),
+            pl.BlockSpec(memory_space=pltpu.HBM),
+            pl.BlockSpec(memory_space=pltpu.HBM),
+            pl.BlockSpec(memory_space=pltpu.HBM),
         ],
         out_specs=pl.BlockSpec(memory_space=pltpu.VMEM),
         scratch_shapes=[
@@ -323,7 +355,7 @@
             pltpu.SemaphoreType.DMA,
         ],
         compiler_params=pltpu.CompilerParams(
-            collective_id=0, has_side_effects=True, vmem_limit_bytes=60 * 2**20
+            collective_id=0, has_side_effects=True, vmem_limit_bytes=40 * 2**20
         ),
     )(offsets, weights, usable_point_flags.T, prediction, observed_state, mean_state)
     return found.reshape(mine, cols, channels)
@@ -336,6 +368,7 @@
         -(-channels // SLOTS) <= n <= channels
         and cols % SLOTS == 0
         and rows % group == 0
+        and n_lon == group
         and (cols * n_lon) % LANES == 0
         and lags % n_lat == 0
         and lags // n_lat * cols <= LANES

time: 45.6 us -> 49 us (1.075)
  local copies, waits for them, and re-layouts: 1.54 us -> 5.15 us
  other arithmetic: 0.56 us -> 0.05 us
    unnamed x1 -> x11, local copies, waits for them, and re-layouts: 1.54 us -> 5.15 us
    cos x1, other arithmetic: 0.56 us -> 0.05 us  [by_channel(): weights = jnp.cos(jnp.pi * ((row_index + 0.5) / total_rows - 0.5))]
where the time goes in v6:
time: 49 us; the launch traced here: 48.7 us
  Pallas kernels  43.5 us (89%)
  local copies, waits for them, and re-layouts  5.15 us (11%)
    pallas_call x1, Pallas kernels, by_channel(): pl.pallas_call(functools.partial(lag_kernel, (n_lat, n_lon, rows, cols, l...  43.5 us
    unnamed x11, local copies, waits for them, and re-layouts  5.15 us

profile of v6, /device:TPU:0, one launch (start us, length us, event | category | flops | bytes accessed | tf_op | source)
XLA Modules:
  0.0 48.7 jit_solution(14258443926635386478)
XLA Ops:
  0.0 0.0 copy-start.4
  0.0 0.6 %copy-done.4 = s32[8]{0:T(128)S(1)} copy-done((s32[8]{0:T(128)S(1)}, s32[8]{0:T(128)}, u32[]{:S(2)}) %copy-start.4) | copy-done | bytes 56
  0.7 0.0 copy-start
  0.7 1.1 %copy-done = bf16[48,24,222]{2,1,0:T(8,128)(2,1)S(1)} copy-done((bf16[48,24,222]{2,1,0:T(8,128)(2,1)S(1)}, bf16[48,24,222]{2,1,0:T(8,128)(2,1)}, u32[]{:S(2)}) %copy-start) | copy-done | bytes 511512
  1.7 0.0 copy-start.1
  1.7 1.1 %copy-done.1 = bf16[48,24,222]{2,1,0:T(8,128)(2,1)S(1)} copy-done((bf16[48,24,222]{2,1,0:T(8,128)(2,1)S(1)}, bf16[48,24,222]{2,1,0:T(8,128)(2,1)}, u32[]{:S(2)}) %copy-start.1) | copy-done | bytes 511512
  2.8 0.0 copy-start.2
  2.8 1.1 %copy-done.2 = bf16[48,24,222]{2,1,0:T(8,128)(2,1)S(1)} copy-done((bf16[48,24,222]{2,1,0:T(8,128)(2,1)S(1)}, bf16[48,24,222]{2,1,0:T(8,128)(2,1)}, u32[]{:S(2)}) %copy-start.2) | copy-done | bytes 511512
  3.9 0.0 copy-start.3
  3.9 0.7 %copy-done.3 = s32[48,24]{0,1:T(8,128)S(1)} copy-done((s32[48,24]{0,1:T(8,128)S(1)}, s32[48,24]{0,1:T(8,128)}, u32[]{:S(2)}) %copy-start.3) | copy-done | bytes 4632
  4.6 43.5 %shard_map.55 = f32[96,222]{1,0:T(8,128)S(1)} custom-call(s32[8]{0:T(128)S(1)} %copy-done.4, f32[96]{0:T(128)S(1)} %multiply_cosine_fusion.weights, s32[24,48]{1,0:T(8,128)S(1)} %bitcast.3, bf16[48,24,222]{2,1,0:T(8,128)(2,1)S(1)} %copy-done, bf16[48,24,222]{2,1,0:T(8,128)(2,1)S(1)} %copy-done.1, bf16[48,24,222]{2,1,0:T(8,128)(2,1)S(1)} %copy-done.2), custom_call_target="tpu_custom_call" | custom-call | tf_op jit(solution)/shard_map/pallas_call | solution.py:326
  48.1 0.6 %copy.7 = f32[4,24,222]{2,1,0:T(8,128)} copy(f32[4,24,222]{2,1,0:T(8,128)S(1)} %bitcast.2) | data formatting | bytes 170496
  (1 shorter events, 0.0 us)
Async XLA Ops:
  0.0 0.7 %copy-start.4 = (s32[8]{0:T(128)S(1)}, s32[8]{0:T(128)}, u32[]{:S(2)}) copy-start(s32[8]{0:T(128)} %offsets.1) | copy-start | bytes 100
  0.7 1.1 %copy-start = (bf16[48,24,222]{2,1,0:T(8,128)(2,1)S(1)}, bf16[48,24,222]{2,1,0:T(8,128)(2,1)}, u32[]{:S(2)}) copy-start(bf16[48,24,222]{2,1,0:T(8,128)(2,1)} %prediction.1) | copy-start | bytes 1534468
  1.7 1.1 %copy-start.1 = (bf16[48,24,222]{2,1,0:T(8,128)(2,1)S(1)}, bf16[48,24,222]{2,1,0:T(8,128)(2,1)}, u32[]{:S(2)}) copy-start(bf16[48,24,222]{2,1,0:T(8,128)(2,1)} %observed.1) | copy-start | bytes 1534468
  2.8 1.1 %copy-start.2 = (bf16[48,24,222]{2,1,0:T(8,128)(2,1)S(1)}, bf16[48,24,222]{2,1,0:T(8,128)(2,1)}, u32[]{:S(2)}) copy-start(bf16[48,24,222]{2,1,0:T(8,128)(2,1)} %mean.1) | copy-start | bytes 1534468
  3.9 0.7 %copy-start.3 = (s32[48,24]{0,1:T(8,128)S(1)}, s32[48,24]{0,1:T(8,128)}, u32[]{:S(2)}) copy-start(s32[48,24]{0,1:T(8,128)} %param.8) | copy-start | bytes 13828

commit v7 on v6

--- a/solution.py
+++ b/solution.py
@@ -3,6 +3,7 @@
 
 import jax
 import jax.numpy as jnp
+import numpy as np
 from jax import lax
 from jax.experimental import pallas as pl
 from jax.experimental.pallas import tpu as pltpu
@@ -46,9 +47,6 @@
 
     def place(rank):
         return {"lat": rank % n_lat, "lon": rank // n_lat}
-
-    def part(b):
-        return pl.ds(pl.multiple_of(b * width, LANES), width)
 
     barrier = pltpu.get_barrier_semaphore()
 
@@ -95,13 +93,13 @@
             ).reshape(groups, SLOTS, width)
             for values in (fore, true)
         ]
-        sent[:, :, b * width : (b + 1) * width] = jnp.concatenate(turned, axis=1).astype(
+        sent[b] = jnp.concatenate(turned, axis=1).astype(
             jnp.bfloat16
         )
 
     def own(b):
         return pltpu.make_async_copy(
-            sent.at[mine, :, part(b)], got.at[me, :, part(b)], own_sem.at[b]
+            sent.at[b, mine], got.at[b, me], own_sem.at[b]
         )
 
     pack(0)
@@ -111,8 +109,8 @@
 
     def outgoing(b, u):
         return pltpu.make_async_remote_copy(
-            src_ref=sent.at[u, :, part(b)],
-            dst_ref=got.at[me, :, part(b)],
+            src_ref=sent.at[b, u],
+            dst_ref=got.at[b, me],
             send_sem=send_sem.at[b, u],
             recv_sem=recv_sem.at[b, me],
             device_id=place(rank_of(u, n, groups)),
@@ -121,8 +119,8 @@
 
     def arriving(b, rank):
         return pltpu.make_async_remote_copy(
-            src_ref=got.at[rank, :, part(b)],
-            dst_ref=got.at[rank, :, part(b)],
+            src_ref=got.at[b, rank],
+            dst_ref=got.at[b, rank],
             send_sem=send_sem.at[b, 0],
             recv_sem=recv_sem.at[b, rank],
             device_id=place(rank),
@@ -162,11 +160,7 @@
         def unpack(half, _):
             chunks = [
                 [
-                    got[
-                        d * n_lat + half,
-                        :,
-                        pl.ds(pl.multiple_of(b * width + m * LANES, LANES), LANES),
-                    ].astype(jnp.float32)
+                    got[b, d * n_lat + half, :, m * LANES : (m + 1) * LANES].astype(jnp.float32)
                     for m in range(tiles)
                 ]
                 for d in range(n_lon)
@@ -315,10 +309,9 @@
     lags = offsets.shape[0]
     n = n_lat * n_lon
     groups = -(-channels // SLOTS)
-    points = rows * cols
     total_rows, total_cols = rows * n_lat, cols * n_lon
-    row_index = jnp.arange(total_rows, dtype=jnp.int32).astype(jnp.float32)
-    weights = jnp.cos(jnp.pi * ((row_index + 0.5) / total_rows - 0.5))
+    latitude = np.pi * ((np.arange(total_rows) + 0.5) / total_rows - 0.5)
+    weights = jnp.asarray(np.cos(latitude), jnp.float32)
     group = math.lcm(cols, LANES) // cols
     phases = rows // group
     held = (n_lat * group, SLOTS, total_cols)
@@ -337,9 +330,9 @@
         out_specs=pl.BlockSpec(memory_space=pltpu.VMEM),
         scratch_shapes=[
             pltpu.VMEM((3, rows, cols, channels), jnp.bfloat16),
-            pltpu.VMEM((groups, 2 * SLOTS, points), jnp.bfloat16),
+            pltpu.VMEM((phases, groups, 2 * SLOTS, group * cols), jnp.bfloat16),
             pltpu.VMEM((groups, SLOTS, LANES), jnp.float32),
-            pltpu.VMEM((n, 2 * SLOTS, points), jnp.bfloat16),
+            pltpu.VMEM((phases, n, 2 * SLOTS, group * cols), jnp.bfloat16),
             pltpu.VMEM(held, jnp.float32),
             pltpu.VMEM(held, jnp.float32),
             pltpu.VMEM(held, jnp.float32),
@@ -355,7 +348,7 @@
             pltpu.SemaphoreType.DMA,
         ],
         compiler_params=pltpu.CompilerParams(
-            collective_id=0, has_side_effects=True, vmem_limit_bytes=40 * 2**20
+            collective_id=0, has_side_effects=True, vmem_limit_bytes=60 * 2**20
         ),
     )(offsets, weights, usable_point_flags.T, prediction, observed_state, mean_state)
     return found.reshape(mine, cols, channels)

time: 49 us -> 46.1 us (0.941)
  local copies, waits for them, and re-layouts: 5.15 us -> 1.54 us
  Pallas kernels: 43.5 us -> 44.3 us
    unnamed x11 -> x1, local copies, waits for them, and re-layouts: 5.15 us -> 1.54 us
    pallas_call x1, Pallas kernels: 43.5 us -> 44.3 us  [by_channel(): pl.pallas_call(functools.partial(lag_kernel, (n_lat, n_lon, rows, cols, l...]
where the time goes in v7:
time: 46.1 us; the launch traced here: 45.8 us
  Pallas kernels  44.3 us (96%)
  local copies, waits for them, and re-layouts  1.54 us (3%)
    pallas_call x1, Pallas kernels, by_channel(): pl.pallas_call(functools.partial(lag_kernel, (n_lat, n_lon, rows, cols, l...  44.3 us
    unnamed x1, local copies, waits for them, and re-layouts  1.54 us

profile of v7, /device:TPU:0, one launch (start us, length us, event | category | flops | bytes accessed | tf_op | source)
XLA Modules:
  0.0 45.8 jit_solution(18101896351942485678)
XLA Ops:
  0.0 44.3 %shard_map.64 = f32[96,222]{1,0:T(8,128)} custom-call(s32[8]{0:T(128)} %offsets.1, f32[96]{0:T(128)} %constant.2.clone.weights, s32[24,48]{1,0:T(8,128)} %bitcast.3, bf16[48,24,222]{2,1,0:T(8,128)(2,1)} %prediction.1, bf16[48,24,222]{2,1,0:T(8,128)(2,1)} %observed.1, bf16[48,24,222]{2,1,0:T(8,128)(2,1)} %mean.1), custom_call_target="tpu_custom_call" | custom-call | tf_op jit(solution)/shard_map/pallas_call | solution.py:319
  44.3 1.5 %copy.8 = f32[4,24,222]{2,1,0:T(8,128)} copy(f32[4,24,222]{2,1,0:T(8,128)} %bitcast.2) | data formatting | bytes 170496

commit v8 on v4

--- a/solution.py
+++ b/solution.py
@@ -3,6 +3,7 @@
 
 import jax
 import jax.numpy as jnp
+import numpy as np
 from jax import lax
 from jax.experimental import pallas as pl
 from jax.experimental.pallas import tpu as pltpu
@@ -245,12 +246,17 @@
                 found[d * n_lat + owner, :, at * cols : (at + 1) * cols] = value[
                     :, d * cols : (d + 1) * cols
                 ]
-
-        def send_back(o, _):
-            returning((me + o) % n).start()
-            return 0
-
-        lax.fori_loop(1, n, send_back, 0)
+            if at == per_owner - 1:
+
+                def send_back(d, _, owner=owner):
+                    @pl.when(d * n_lat + owner != me)
+                    def _():
+                        returning(d * n_lat + owner).start()
+
+                    return 0
+
+                lax.fori_loop(0, n_lon, send_back, 0)
+
         last.start()
 
         def sent_back(o, _):
@@ -285,8 +291,8 @@
     groups = -(-channels // SLOTS)
     points = rows * cols
     total_rows, total_cols = rows * n_lat, cols * n_lon
-    row_index = jnp.arange(total_rows, dtype=jnp.int32).astype(jnp.float32)
-    weights = jnp.cos(jnp.pi * ((row_index + 0.5) / total_rows - 0.5))
+    latitude = np.pi * ((np.arange(total_rows) + 0.5) / total_rows - 0.5)
+    weights = jnp.asarray(np.cos(latitude), jnp.float32)
     group = math.lcm(cols, LANES) // cols
     phases = rows // group
     held = (n_lat * group, SLOTS, total_cols)

time: 45.6 us -> 44.6 us (0.978)
  other arithmetic: 0.56 us -> 0 us
  Pallas kernels: 43.3 us -> 42.8 us
    cos x1 -> x0, other arithmetic: 0.56 us -> none  [by_channel(): weights = jnp.cos(jnp.pi * ((row_index + 0.5) / total_rows - 0.5))]
    pallas_call x1, Pallas kernels: 43.3 us -> 42.8 us  [by_channel(): pl.pallas_call(functools.partial(lag_kernel, (n_lat, n_lon, rows, cols, l...]
where the time goes in v8:
time: 44.6 us; the launch traced here: 44.4 us
  Pallas kernels  42.8 us (96%)
  local copies, waits for them, and re-layouts  1.54 us (3%)
    pallas_call x1, Pallas kernels, by_channel(): pl.pallas_call(functools.partial(lag_kernel, (n_lat, n_lon, rows, cols, l...  42.8 us
    unnamed x1, local copies, waits for them, and re-layouts  1.54 us

profile of v8, /device:TPU:0, one launch (start us, length us, event | category | flops | bytes accessed | tf_op | source)
XLA Modules:
  0.0 44.4 jit_solution(6051426128298851789)
XLA Ops:
  0.0 42.8 %shard_map.64 = f32[96,222]{1,0:T(8,128)} custom-call(s32[8]{0:T(128)} %offsets.1, f32[96]{0:T(128)} %constant.2.clone.weights, s32[24,48]{1,0:T(8,128)} %bitcast.3, bf16[48,24,222]{2,1,0:T(8,128)(2,1)} %prediction.1, bf16[48,24,222]{2,1,0:T(8,128)(2,1)} %observed.1, bf16[48,24,222]{2,1,0:T(8,128)(2,1)} %mean.1), custom_call_target="tpu_custom_call" | custom-call | tf_op jit(solution)/shard_map/pallas_call | solution.py:300
  42.8 1.5 %copy.8 = f32[4,24,222]{2,1,0:T(8,128)} copy(f32[4,24,222]{2,1,0:T(8,128)} %bitcast.2) | data formatting | bytes 170496
